TPU v7x, 128 devices: a whole 4x4x4 slice. The times are simulated.
128 devices in a mesh: region: 8 (over z_hi, y), group: 16 (over x, z_lo, core).
Axes of the slice: x: 4, y: 4, z: 4 (z_hi: 2, z_lo: 2; z = z_hi * 2 + z_lo), core: 2. Of those that a mesh axis runs over, the one named last changes fastest.
Arguments:
- tracers: float32 [32, 32, 64, 512], P('group', None, 'region'), may hold values from -6 to 6
- velocity: float32 [3, 32, 64, 512], P(None, None, 'region', 'group'), may hold values from -0.3 to 0.3
- sea_mask: int32 [32, 64, 512], P(None, 'region'), may hold values 0 or 1
- coupling: float32 [32, 32], replicated, may hold values from -1 to 1
- mixing: float32 [32], replicated, may hold values from 0.05 to 0.2
Outputs:
- fields: float32 [32, 32, 64, 512], P('group', None, 'region')
Inputs may be any that keep to these rules, and one draw needn't show every extreme that they name: `sea_mask`: 1 marks an ocean cell, 0 land.
All inputs are finite; a program needn't handle non-finite values. No bound on the sum of `sea_mask` on one device may be relied on, other than what follows from the above.
Results may differ from a plain program's by a relative error of at most 0.0003.
Values sent between devices are 32-bit elements; how exact they have to be, the bound alone decides.
A program may use at most 128 MiB of HBM per device.

v0:
```python
import functools

import jax
import jax.numpy as jnp
import numpy as np
from jax import lax
from jax.experimental import pallas as pl
from jax.experimental.pallas import tpu as pltpu
from jax.sharding import PartitionSpec as P

MESH = pl.DeviceIdType.MESH
STEPS = 2
NZ, NT, X, YB, G, R = 32, 32, 8, 32, 16, 8
XE, YE = X + 4, YB + 4
QUADS = ((0, 1, 6, 7), (2, 3, 4, 5))
NC = 10
OX, CX, QX, OY, CY, QY, OZ, CZ, QZ, SEA = range(NC)


def minmod(a, b):
    return jnp.maximum(jnp.minimum(a, b), jnp.minimum(jnp.maximum(a, b), 0.0))


def face(cell, following, slope, slope_following, c, q):
    forward = c > 0
    return c * (jnp.where(forward, cell, following) + q * jnp.where(forward, slope, slope_following))


def halves(value):
    high = value.astype(jnp.bfloat16)
    return high, (value - high.astype(jnp.float32)).astype(jnp.bfloat16)


def block_swap(v, lane):
    low, even = lane < 64, (lane // 32) % 2 == 0
    axis = v[0].ndim - 1
    a = [None] * 4
    for n in (0, 1):
        a[n] = jnp.where(low, v[n], pltpu.roll(v[n + 2], 64, axis))
        a[n + 2] = jnp.where(low, pltpu.roll(v[n], 64, axis), v[n + 2])
    b = [None] * 4
    for n in (0, 2):
        b[n] = jnp.where(even, a[n], pltpu.roll(a[n + 1], 32, axis))
        b[n + 1] = jnp.where(even, pltpu.roll(a[n], 96, axis), a[n + 1])
    return b


def kernel(tr, coef_in, spread, weights, own_mat, past_mat, mix, out,
           wmat, tin, tout, sb, rb, fa, fb, adv, coef, so, ro,
           tiles_in, tiles_out, send_in, recv_in, send_halo, recv_x, recv_y, send_out, recv_out, local_sem):
    r, g = lax.axis_index("region"), lax.axis_index("group")
    lane = lax.broadcasted_iota(jnp.int32, (8, 128), 1)
    row = lax.broadcasted_iota(jnp.int32, (8, 128), 0)
    fa2, fb2 = fa.reshape(XE * YE * 8, 128), fb.reshape(XE * YE * 8, 128)
    rb2, so2 = rb.reshape(2 * 4 * NT * 8, 128), so.reshape(2 * 4 * NT * 8, 128)

    def fetch(j):
        return pltpu.make_async_copy(tr.at[:, pl.ds(j * 128, 128)], tin.at[j], tiles_in.at[j])

    def put(j):
        return pltpu.make_async_copy(tout.at[j], out.at[:, pl.ds(j * 128, 128)], tiles_out.at[j])

    for j in range(4):
        fetch(j).start()

    for f in (fa, fb):
        f[0:2, 2:34] = jnp.zeros((2, 32, 8, 128), jnp.float32)
        f[10:12, 2:34] = jnp.zeros((2, 32, 8, 128), jnp.float32)
        f[2:10, 0:2] = jnp.zeros((8, 2, 8, 128), jnp.float32)
        f[2:10, 34:36] = jnp.zeros((8, 2, 8, 128), jnp.float32)

    barrier = pltpu.get_barrier_semaphore()

    def greet(d, carry):
        pl.semaphore_signal(barrier, inc=1, device_id=(r, lax.rem(g + d, G)), device_id_type=MESH)
        return carry

    lax.fori_loop(1, G, greet, 0)

    @pl.when(r > 0)
    def _():
        pl.semaphore_signal(barrier, inc=1, device_id=(r - 1, g), device_id_type=MESH)

    @pl.when(r < R - 1)
    def _():
        pl.semaphore_signal(barrier, inc=1, device_id=(r + 1, g), device_id_type=MESH)

    for j in range(4):
        fetch(j).wait()

    for h, quad in enumerate(QUADS):
        def regroup(n, carry, h=h, quad=quad):
            t, zq = n // 4, n % 4
            for j in range(4):
                v = [tin[j, pl.ds((t * NZ + zq * 8) * X + x, 8, stride=8), :] for x in quad]
                for i, b in enumerate(block_swap(v, lane)):
                    sb[4 * j + i, h, zq, t] = b
            return carry

        lax.fori_loop(0, 8, regroup, 0)
        if h == 0:
            pl.semaphore_wait(barrier, G - 1 + jnp.minimum(r, 1) + jnp.minimum(R - 1 - r, 1))

        def send(d, carry, h=h):
            to = lax.rem(g + d, G)
            pltpu.make_async_remote_copy(
                src_ref=sb.at[to, h], dst_ref=rb.at[h, :, pl.ds(2 * g, 2)],
                send_sem=send_in.at[h], recv_sem=recv_in.at[h],
                device_id=(r, to), device_id_type=MESH).start()
            return carry

        lax.fori_loop(1, G, send, 0)
        pltpu.make_async_copy(sb.at[g, h], rb.at[h, :, pl.ds(2 * g, 2)], local_sem.at[h]).start()

    high, low = halves(weights[...])
    wmat[...] = jnp.concatenate([jnp.concatenate([high, low], 1), jnp.concatenate([high, jnp.zeros_like(low)], 1)], 0)

    def spread_one(zr, carry):
        d = coef_in[zr]
        high = d.astype(jnp.bfloat16).astype(jnp.float32)
        rest = d - high
        mid = rest.astype(jnp.bfloat16).astype(jnp.float32)
        low = rest - mid
        stack = jnp.concatenate([high, mid, low, jnp.zeros((8, 512), jnp.float32)], axis=0)
        turned = stack.T.astype(jnp.bfloat16)
        for k in range(NC):
            wide = jnp.dot(turned, spread[k], preferred_element_type=jnp.float32)
            coef.at[k].reshape(XE * YE * 8, 128)[pl.ds(zr, XE * YE, stride=8), :] = wide[:XE * YE]
        return carry

    lax.fori_loop(0, 8, spread_one, 0)

    def x_halo(f, s, do):
        @pl.when(r > 0)
        def _():
            do(pltpu.make_async_remote_copy(
                src_ref=f.at[2:4, 2:34], dst_ref=f.at[10:12, 2:34],
                send_sem=send_halo.at[s, 0], recv_sem=recv_x.at[s, 1],
                device_id=(r - 1, g), device_id_type=MESH))

        @pl.when(r < R - 1)
        def _():
            do(pltpu.make_async_remote_copy(
                src_ref=f.at[8:10, 2:34], dst_ref=f.at[0:2, 2:34],
                send_sem=send_halo.at[s, 1], recv_sem=recv_x.at[s, 0],
                device_id=(r + 1, g), device_id_type=MESH))

    def y_halo(f, s, do):
        @pl.when(g > 0)
        def _():
            do(pltpu.make_async_remote_copy(
                src_ref=f.at[2:10, 2:4], dst_ref=f.at[2:10, 34:36],
                send_sem=send_halo.at[s, 2], recv_sem=recv_y.at[s, 1],
                device_id=(r, g - 1), device_id_type=MESH))

        @pl.when(g < G - 1)
        def _():
            do(pltpu.make_async_remote_copy(
                src_ref=f.at[2:10, 32:34], dst_ref=f.at[2:10, 0:2],
                send_sem=send_halo.at[s, 3], recv_sem=recv_y.at[s, 0],
                device_id=(r, g + 1), device_id_type=MESH))

    def begin(copy):
        copy.start()

    def arrive(f, s):
        def landed(ref, sem):
            pltpu.make_async_copy(ref, ref, sem).wait()

        @pl.when(r > 0)
        def _():
            landed(f.at[0:2, 2:34], recv_x.at[s, 0])

        @pl.when(r < R - 1)
        def _():
            landed(f.at[10:12, 2:34], recv_x.at[s, 1])

        @pl.when(g > 0)
        def _():
            landed(f.at[2:10, 0:2], recv_y.at[s, 0])

        @pl.when(g < G - 1)
        def _():
            landed(f.at[2:10, 34:36], recv_y.at[s, 1])

    for h, quad in enumerate(QUADS):
        some = rb.at[h, :, 0:2 * (G - 1)]
        pltpu.make_async_copy(some, some, recv_in.at[h]).wait()
        pltpu.make_async_copy(sb.at[g, h], rb.at[h, :, pl.ds(2 * g, 2)], local_sem.at[h]).wait()

        def turn(zr, carry, h=h, quad=quad):
            turned = rb2[pl.ds(h * 4 * NT * 8 + zr, 128, stride=8), :].T
            for n, x in enumerate(quad):
                fa2[pl.ds(((x + 2) * YE + 2) * 8 + zr, YB, stride=8), :] = turned[n * YB:(n + 1) * YB]
            return carry

        lax.fori_loop(0, 8, turn, 0)
        if h == 0:
            x_halo(fa, 0, begin)
    y_halo(fa, 0, begin)

    def z_up(v):
        s = pltpu.roll(v, 7, 1)
        return jnp.where(row == 7, pltpu.roll(s, 96, 2), s)

    def z_down(v):
        s = pltpu.roll(v, 1, 1)
        return jnp.where(row == 0, pltpu.roll(s, 32, 2), s)

    def advect(f):
        def cells(e):
            return f[2:10, e]

        def along(k, e):
            return coef[k, 2:10, e]

        f1, f2 = cells(1), cells(2)
        j0 = (f1 - cells(0)) * along(OY, 0)
        j1 = (f2 - f1) * along(OY, 1)
        j2 = (cells(3) - f2) * along(OY, 2)
        s1, s2 = minmod(j0, j1), minmod(j1, j2)
        start = (j2, s2, face(f1, f2, s1, s2, along(CY, 1), along(QY, 1)))

        def column(y, carry):
            jump, slope, before = carry
            e = y + 2
            fx = f[:, e]
            inner, following = fx[2:10], cells(e + 1)
            jump_next = (cells(e + 2) - following) * along(OY, e + 1)
            slope_next = minmod(jump, jump_next)
            after = face(inner, following, slope, slope_next, along(CY, e), along(QY, e))
            total = inner - (after - before)
            jx = (fx[1:] - fx[:-1]) * coef[OX, 0:11, e]
            sx = minmod(jx[:-1], jx[1:])
            flux = face(fx[1:10], fx[2:11], sx[:-1], sx[1:], coef[CX, 1:10, e], coef[QX, 1:10, e])
            total = total - (flux[1:] - flux[:-1])
            below = z_up(inner)
            jz = (below - inner) * along(OZ, e)
            sz = minmod(z_down(jz), jz)
            down = face(inner, below, sz, z_up(sz), along(CZ, e), along(QZ, e)) - mix[...] * jz
            adv[:, y] = total - (down - z_down(down))
            return jump_next, slope_next, after

        lax.fori_loop(0, YB, column, start)

    def react(x, f):
        a = adv[x]
        att = 0.05 + 0.1 * a * a
        inc = att
        for step in (1, 2, 4):
            inc = inc + jnp.where(row >= step, pltpu.roll(inc, step, 1), 0.0)
        exc = (inc - att).reshape(256, 128)
        ahead = jnp.dot(jnp.concatenate(halves(exc), axis=1), own_mat[...], preferred_element_type=jnp.float32)
        past = jnp.dot(jnp.concatenate(halves(inc.reshape(256, 128)), axis=1), past_mat[...],
                       preferred_element_type=jnp.float32).reshape(YB, 8, 128)
        light = jnp.exp(-(ahead.reshape(YB, 8, 128) + past[:, 7:8, :]))
        both = jnp.dot(jnp.concatenate(halves(jnp.tanh(a).reshape(256, 128)), axis=1), wmat[...],
                       preferred_element_type=jnp.float32)
        response = (both[:, :128] + both[:, 128:]).reshape(YB, 8, 128)
        f[x + 2, 2:34] = a + coef[SEA, x + 2, 2:34] * ((0.5 + light) * response)

    arrive(fa, 0)
    advect(fa)
    for h, quad in enumerate(QUADS):
        for x in quad:
            react(x, fb)
        if h == 0:
            x_halo(fb, 1, begin)
    y_halo(fb, 1, begin)
    arrive(fb, 1)
    advect(fb)
    for s, f in ((0, fa), (1, fb)):
        x_halo(f, s, lambda copy: copy.wait_send())
        y_halo(f, s, lambda copy: copy.wait_send())

    for h, quad in enumerate(QUADS):
        for x in quad:
            react(x, fa)

        def turn_back(zr, carry, h=h, quad=quad):
            stack = [fa2[pl.ds(((x + 2) * YE + 2) * 8 + zr, YB, stride=8), :] for x in quad]
            so2[pl.ds(h * 4 * NT * 8 + zr, 128, stride=8), :] = jnp.concatenate(stack, axis=0).T
            return carry

        lax.fori_loop(0, 8, turn_back, 0)

        def send_back(d, carry, h=h):
            to = lax.rem(g + d, G)
            pltpu.make_async_remote_copy(
                src_ref=so.at[h, :, pl.ds(2 * to, 2)], dst_ref=ro.at[h, g],
                send_sem=send_out.at[h], recv_sem=recv_out.at[h],
                device_id=(r, to), device_id_type=MESH).start()
            return carry

        lax.fori_loop(1, G, send_back, 0)
        pltpu.make_async_copy(so.at[h, :, pl.ds(2 * g, 2)], ro.at[h, g], local_sem.at[2 + h]).start()

    for h, quad in enumerate(QUADS):
        some = ro.at[h, 0:G - 1]
        pltpu.make_async_copy(some, some, recv_out.at[h]).wait()
        pltpu.make_async_copy(so.at[h, :, pl.ds(2 * g, 2)], ro.at[h, g], local_sem.at[2 + h]).wait()

        def restore(n, carry, h=h, quad=quad):
            t, zq = n // 4, n % 4
            for j in range(4):
                v = block_swap([ro[h, 4 * j + i, zq, t] for i in range(4)], lane)
                for x, b in zip(quad, v):
                    tout[j, pl.ds((t * NZ + zq * 8) * X + x, 8, stride=8), :] = b
            return carry

        lax.fori_loop(0, 8, restore, 0)

    for j in range(4):
        put(j).start()
    for h in range(2):
        some = sb.at[0:G - 1, h]
        pltpu.make_async_copy(some, some, send_in.at[h]).wait()
        some = ro.at[h, 0:G - 1]
        pltpu.make_async_copy(some, some, send_out.at[h]).wait()
    for j in range(4):
        put(j).wait()


def neighbours(value, axis, shift):
    size = lax.axis_size(axis)
    pairs = [(i, i + shift) for i in range(size) if 0 <= i + shift < size]
    return lax.ppermute(value, axis, pairs)


def face_coefficients(velocity, sea_mask, coupling):
    g = lax.axis_index("group")
    sea = jnp.pad(sea_mask.astype(jnp.float32), ((0, 0), (0, 0), (2, 2)))
    sea = lax.dynamic_slice_in_dim(sea, g * YB, YE, axis=2)
    vx, vy, vz = velocity[0], velocity[1], velocity[2]
    low = neighbours(jnp.concatenate([sea[:, 6:8, 2:34], vx[:, 7:8]], axis=1), "region", 1)
    high = neighbours(sea[:, 0:2, 2:34], "region", -1)
    vy_low = neighbours(vy[:, :, 31:32], "group", 1)
    edges = ((0, 0), (0, 0), (2, 2))
    sea = jnp.concatenate([jnp.pad(low[:, 0:2], edges), sea, jnp.pad(high, edges)], axis=1)
    vx = jnp.pad(jnp.concatenate([low[:, 2:3], vx], axis=1), ((0, 0), (1, 2), (2, 2)))
    vy = jnp.pad(jnp.concatenate([vy_low, vy], axis=2), ((0, 0), (2, 2), (1, 2)))
    vz = jnp.pad(vz, ((0, 0), (2, 2), (2, 2)))
    ends = [(0, 0)] * 3
    parts = []
    for axis, c in ((1, vx), (2, vy), (0, vz)):
        pad = [(0, 1) if n == axis else (0, 0) for n in range(3)]
        following = jnp.pad(lax.slice_in_dim(sea, 1, sea.shape[axis], axis=axis), pad)
        opened = sea * following
        parts += [opened, c * opened, 0.5 * jnp.sign(c) - 0.5 * c]
    parts.append(sea)
    whole = jnp.stack(parts, 0).reshape(NC, 4, 8, XE * YE)
    whole = jnp.moveaxis(whole, 2, 0).reshape(8, NC * 4, XE * YE)
    return jnp.pad(whole, ((0, 0), (0, 0), (0, 512 - XE * YE)))


def shards(tracers, velocity, sea_mask, coupling, mixing):
    coef_in = face_coefficients(velocity, sea_mask, coupling)
    spread = np.zeros((NC, 3, NC, 4, 4, NT), np.float32)
    for k in range(NC):
        for b in range(4):
            spread[k, :, k, b, b] = 1
    spread = np.pad(spread.reshape(NC, 3 * NC * 4, 128), ((0, 0), (0, 8), (0, 0)))
    own = np.zeros((4, NT, 4, NT), np.float32)
    past = np.zeros((4, NT, 4, NT), np.float32)
    for a in range(4):
        own[a, 0, a] = 1
        past[a, 0, a + 1:] = 1
    own, past = own.reshape(128, 128), past.reshape(128, 128)
    own, past = np.concatenate([own, own], 0), np.concatenate([past, past], 0)
    block = np.kron(np.eye(4, dtype=np.float32), np.ones((NT, NT), np.float32))
    weights = jnp.tile(coupling.T, (4, 4)) * block
    mix = jnp.broadcast_to(mixing.reshape(4, 8).T[:, :, None], (8, 4, NT)).reshape(8, 128)

    vmem = pl.BlockSpec(memory_space=pltpu.VMEM)
    f32 = jnp.float32
    dma = pltpu.SemaphoreType.DMA
    out = pl.pallas_call(
        kernel,
        out_shape=jax.ShapeDtypeStruct((2 * NZ * X, G * YB), f32),
        in_specs=[pl.BlockSpec(memory_space=pl.ANY)] + [vmem] * 6,
        out_specs=pl.BlockSpec(memory_space=pl.ANY),
        scratch_shapes=[
            pltpu.VMEM((256, 256), jnp.bfloat16),
            pltpu.VMEM((4, 2 * NZ * X, 128), f32),
            pltpu.VMEM((4, 2 * NZ * X, 128), f32),
            pltpu.VMEM((G, 2, 4, 2, 8, 128), f32),
            pltpu.VMEM((2, 4, NT, 8, 128), f32),
            pltpu.VMEM((XE, YE, 8, 128), f32),
            pltpu.VMEM((XE, YE, 8, 128), f32),
            pltpu.VMEM((X, YB, 8, 128), f32),
            pltpu.VMEM((NC, XE, YE, 8, 128), f32),
            pltpu.VMEM((2, 4, NT, 8, 128), f32),
            pltpu.VMEM((2, G, 4, 2, 8, 128), f32),
            dma((4,)), dma((4,)), dma((2,)), dma((2,)), dma((2, 4)), dma((2, 2)), dma((2, 2)), dma((2,)), dma((2,)), dma((4,)),
        ],
        compiler_params=pltpu.CompilerParams(
            collective_id=0, has_side_effects=True, vmem_limit_bytes=48 * 2**20),
    )(tracers.reshape(2 * NZ * X, G * YB), coef_in,
      jnp.asarray(spread, jnp.bfloat16), weights, jnp.asarray(own, jnp.bfloat16),
      jnp.asarray(past, jnp.bfloat16), mix)
    return out.reshape(tracers.shape)


def solution(mesh):
    placed = (
        P("group", None, "region", None),
        P(None, None, "region", "group"),
        P(None, "region", None),
        P(),
        P(),
    )
    return jax.shard_map(
        shards,
        mesh=mesh,
        in_specs=placed,
        out_specs=P("group", None, "region", None),
        check_vma=False,
    )
```

profile of v0, /device:TPU:57, one launch (start us, length us, event | category | flops | bytes accessed | tf_op | source)
XLA Modules:
  0.0 93.5 jit_solution(11653487676066749114)
XLA Ops:
  0.0 1.4 %copy_convert_fusion = f32[32,8,512]{2,0,1:T(8,128)S(1)} fusion(s32[32,8,512]{2,1,0:T(8,128)} %param.11), kind=kLoop, calls=%fused_computation.3 | loop fusion | flops 131072 | bytes 1048576 | tf_op jit(solution)/shard_map/convert_element_type | solution.py:332
  1.6 4.3 %collective-permute-start = (f32[32,3,32]{2,0,1:T(8,128)S(1)}, f32[32,3,32]{2,0,1:T(8,128)S(1)}, u32[]{:S(2)}, u32[]{:S(2)}) collective-permute-start(f32[32,3,32]{2,0,1:T(8,128)S(1)} %pad_maximum_fusion), channel_id=1, source_target_pairs={{0,16},{16,32},{32,48},{48,64},{64,80},{80,96},{96,112},{1,17},{17... | collective-permute-start | bytes 36872 | tf_op jit(solution)/shard_map/ppermute | solution.py:327
  5.9 1.9 %collective-permute-start.1 = (f32[32,2,32]{2,0,1:T(8,128)S(1)}, f32[32,2,32]{2,0,1:T(8,128)S(1)}, u32[]{:S(2)}, u32[]{:S(2)}) collective-permute-start(f32[32,2,32]{2,0,1:T(8,128)S(1)} %get-tuple-element.11), channel_id=1, source_target_pairs={{16,0},{32,16},{48,32},{64,48},{80,64},{96,80},{112,96},{17,1},{33... | collective-permute-start | bytes 24584 | tf_op jit(solution)/shard_map/ppermute | solution.py:327
  7.9 4.4 %collective-permute-start.2 = (f32[32,8,1]{2,0,1:T(8,128)S(1)}, f32[32,8,1]{2,0,1:T(8,128)S(1)}, u32[]{:S(2)}, u32[]{:S(2)}) collective-permute-start(f32[32,8,1]{2,0,1:T(8,128)S(1)} %slice.53), channel_id=1, source_target_pairs={{0,1},{1,2},{2,3},{3,4},{4,5},{5,6},{6,7},{7,8},{8,9},{9,10},{10,1... | collective-permute-start | bytes 3080 | tf_op jit(solution)/shard_map/ppermute | solution.py:327
  12.5 0.6 copy-done.6
  13.5 0.1 copy.37
  13.6 0.1 stack.41
  13.8 0.2 reshape.44.weights
  13.9 0.5 copy-done.7
  14.7 0.1 multiply_subtract_fusion.1
  15.2 0.1 copy.38
  15.3 0.2 fusion.9
  15.6 0.1 copy.27
  15.7 0.1 stack.33
  15.8 0.1 copy.28
  15.9 0.1 stack.34
  16.1 0.1 copy.29
  16.2 0.1 stack.35
  16.3 0.1 copy.30
  16.5 0.1 stack.36
  16.6 0.1 copy.32
  16.7 0.1 stack.37
  16.9 0.1 copy.33
  17.0 0.1 stack.38
  17.2 0.1 stack.39
  17.5 0.1 stack.40
  17.6 0.1 stack.42
  17.9 0.4 copy.42
  18.4 0.7 copy-done
  19.1 0.2 copy-done.1
  19.3 73.2 %shard_map.91 = f32[512,512]{1,0:T(8,128)S(1)} custom-call(f32[512,512]{1,0:T(8,128)S(1)} %bitcast.17, f32[8,40,512]{2,1,0:T(8,128)S(1)} %pad.48.coef_in, bf16[10,128,128]{2,1,0:T(8,128)(2,1)S(1)} %copy-done.1, f32[128,128]{1,0:T(8,128)S(1)} %reshape.44.weights, bf16[256,128]{1,0:T(8,128)(2,1)S(1)} %copy-done.2, bf16[256,128]{1,0:T(8,128)(2,1)S(1)} %copy-done.3, ...), custom_call_target="tpu_custom_call" | custom-call | tf_op jit(solution)/shard_map/pallas_call | solution.py:377
  92.6 1.0 %copy.63 = f32[2,32,8,512]{3,2,1,0:T(8,128)} copy(f32[2,32,8,512]{3,2,1,0:T(8,128)S(1)} %bitcast.16) | data formatting | bytes 2097152
  (50 shorter events, 1.7 us)
Async XLA Ops:
  0.0 1.4 %copy-start.4 = (f32[3,32,8,32]{3,2,1,0:T(8,128)S(1)}, f32[3,32,8,32]{3,2,1,0:T(8,128)}, u32[]{:S(2)}) copy-start(f32[3,32,8,32]{3,2,1,0:T(8,128)} %param.10) | copy-start | bytes 294916
  1.6 13.1 %collective-permute-start = (f32[32,3,32]{2,0,1:T(8,128)S(1)}, f32[32,3,32]{2,0,1:T(8,128)S(1)}, u32[]{:S(2)}, u32[]{:S(2)}) collective-permute-start(f32[32,3,32]{2,0,1:T(8,128)S(1)} %pad_maximum_fusion), channel_id=1, source_target_pairs={{0,16},{16,32},{32,48},{48,64},{64,80},{80,96},{96,112},{1,17},{17... | collective-permute-start | bytes 36872 | tf_op jit(solution)/shard_map/ppermute | solution.py:327
  5.9 9.0 %collective-permute-start.1 = (f32[32,2,32]{2,0,1:T(8,128)S(1)}, f32[32,2,32]{2,0,1:T(8,128)S(1)}, u32[]{:S(2)}, u32[]{:S(2)}) collective-permute-start(f32[32,2,32]{2,0,1:T(8,128)S(1)} %get-tuple-element.11), channel_id=1, source_target_pairs={{16,0},{32,16},{48,32},{64,48},{80,64},{96,80},{112,96},{17,1},{33... | collective-permute-start | bytes 24584 | tf_op jit(solution)/shard_map/ppermute | solution.py:327
  7.9 7.3 %collective-permute-start.2 = (f32[32,8,1]{2,0,1:T(8,128)S(1)}, f32[32,8,1]{2,0,1:T(8,128)S(1)}, u32[]{:S(2)}, u32[]{:S(2)}) collective-permute-start(f32[32,8,1]{2,0,1:T(8,128)S(1)} %slice.53), channel_id=1, source_target_pairs={{0,1},{1,2},{2,3},{3,4},{4,5},{5,6},{6,7},{7,8},{8,9},{9,10},{10,1... | collective-permute-start | bytes 3080 | tf_op jit(solution)/shard_map/ppermute | solution.py:327
  12.4 1.0 %copy-start.5 = (f32[4,32,4,32]{3,2,1,0:T(4,128)S(1)}, f32[4,32,4,32]{3,2,1,0:T(4,128)}, u32[]{:S(2)}) copy-start(f32[4,32,4,32]{3,2,1,0:T(4,128)} %constant.47) | copy-start | bytes 196612
  12.4 0.8 copy-start.6
  13.7 0.7 copy-start.7
  17.9 1.2 %copy-start = (f32[2,32,8,512]{3,2,1,0:T(8,128)S(1)}, f32[2,32,8,512]{3,2,1,0:T(8,128)}, u32[]{:S(2)}) copy-start(f32[2,32,8,512]{3,2,1,0:T(8,128)} %param.9) | copy-start | bytes 3145732
  18.3 1.1 %copy-start.1 = (bf16[10,128,128]{2,1,0:T(8,128)(2,1)S(1)}, bf16[10,128,128]{2,1,0:T(8,128)(2,1)}, u32[]{:S(2)}) copy-start(bf16[10,128,128]{2,1,0:T(8,128)(2,1)} %constant.23.clone.spread) | copy-start | bytes 983044
  18.3 1.0 %copy-start.2 = (bf16[256,128]{1,0:T(8,128)(2,1)S(1)}, bf16[256,128]{1,0:T(8,128)(2,1)}, u32[]{:S(2)}) copy-start(bf16[256,128]{1,0:T(8,128)(2,1)} %constant.24.clone.own_mat) | copy-start | bytes 196612
  18.3 1.0 %copy-start.3 = (bf16[256,128]{1,0:T(8,128)(2,1)S(1)}, bf16[256,128]{1,0:T(8,128)(2,1)}, u32[]{:S(2)}) copy-start(bf16[256,128]{1,0:T(8,128)(2,1)} %constant.25.clone.past_mat) | copy-start | bytes 196612
where the time goes:
time: 93.8 us; the launch traced here: 93.5 us
  Pallas kernels  73.2 us (78%)
  starting transfers between devices  10.6 us (11%)
  local copies, waits for them, and re-layouts  7.26 us (8%)
  other arithmetic  2.05 us (2%)
    pallas_call x1, Pallas kernels, shards(): pl.pallas_call(kernel, out_shape=jax.ShapeDtypeStruct((2 * NZ * X, G * YB...  73.2 us
    ppermute x3, starting transfers between devices, neighbours(): return lax.ppermute(value, axis, pairs)  10.6 us
    unnamed x29, local copies, waits for them, and re-layouts  3.3 us
  transfers between devices with their start and end apart: 3, of which 0 were waited for; matrix products, arithmetic and copies ran while one was open for 2% of the time, Pallas kernels for 0%

commit v1 on v0

--- a/solution.py
+++ b/solution.py
@@ -46,7 +46,7 @@
 
 
 def kernel(tr, coef_in, spread, weights, own_mat, past_mat, mix, out,
-           wmat, tin, tout, sb, rb, fa, fb, adv, coef, so, ro,
+           wmat, tin, tout, sb, rb, fa, fb, adv, edge, coef, so, ro,
            tiles_in, tiles_out, send_in, recv_in, send_halo, recv_x, recv_y, send_out, recv_out, local_sem):
     r, g = lax.axis_index("region"), lax.axis_index("group")
     lane = lax.broadcasted_iota(jnp.int32, (8, 128), 1)
@@ -199,15 +199,26 @@
             x_halo(fa, 0, begin)
     y_halo(fa, 0, begin)
 
-    def z_up(v):
-        s = pltpu.roll(v, 7, 1)
-        return jnp.where(row == 7, pltpu.roll(s, 96, 2), s)
-
-    def z_down(v):
-        s = pltpu.roll(v, 1, 1)
-        return jnp.where(row == 0, pltpu.roll(s, 32, 2), s)
+    def z_edges(f):
+        def rows(ref, k):
+            return ref.reshape(ref.shape[0] * ref.shape[1] * 8, 128)[pl.ds(2 * YE * 8 + k, X * YE, stride=8), :]
+
+        def static(k, n):
+            return rows(coef.at[k], n)
+
+        next0 = pltpu.roll(rows(f, 0), 96, 1)
+        next1 = pltpu.roll(rows(f, 1), 96, 1)
+        last = rows(f, 7)
+        jump = (next0 - last) * static(OZ, 7)
+        slope = minmod((last - rows(f, 6)) * static(OZ, 6), jump)
+        slope_next = minmod(jump, (next1 - next0) * pltpu.roll(static(OZ, 0), 96, 1))
+        flux = face(last, next0, slope, slope_next, static(CZ, 7), static(QZ, 7)) - mix[7:8, :] * jump
+        for n, k, v in ((0, 7, next0), (0, 0, pltpu.roll(jump, 32, 1)), (1, 7, slope_next), (1, 0, pltpu.roll(flux, 32, 1))):
+            edge.at[n].reshape(X * YE * 8, 128)[pl.ds(k, X * YE, stride=8), :] = v
 
     def advect(f):
+        z_edges(f)
+
         def cells(e):
             return f[2:10, e]
 
@@ -234,11 +245,13 @@
             sx = minmod(jx[:-1], jx[1:])
             flux = face(fx[1:10], fx[2:11], sx[:-1], sx[1:], coef[CX, 1:10, e], coef[QX, 1:10, e])
             total = total - (flux[1:] - flux[:-1])
-            below = z_up(inner)
+            edge0, edge1 = edge[0, :, e], edge[1, :, e]
+            below = jnp.where(row == 7, edge0, pltpu.roll(inner, 7, 1))
             jz = (below - inner) * along(OZ, e)
-            sz = minmod(z_down(jz), jz)
-            down = face(inner, below, sz, z_up(sz), along(CZ, e), along(QZ, e)) - mix[...] * jz
-            adv[:, y] = total - (down - z_down(down))
+            sz = minmod(jnp.where(row == 0, edge0, pltpu.roll(jz, 1, 1)), jz)
+            sz_next = jnp.where(row == 7, edge1, pltpu.roll(sz, 7, 1))
+            down = face(inner, below, sz, sz_next, along(CZ, e), along(QZ, e)) - mix[...] * jz
+            adv[:, y] = total - (down - jnp.where(row == 0, edge1, pltpu.roll(down, 1, 1)))
             return jump_next, slope_next, after
 
         lax.fori_loop(0, YB, column, start)
@@ -388,6 +401,7 @@
             pltpu.VMEM((XE, YE, 8, 128), f32),
             pltpu.VMEM((XE, YE, 8, 128), f32),
             pltpu.VMEM((X, YB, 8, 128), f32),
+            pltpu.VMEM((2, X, YE, 8, 128), f32),
             pltpu.VMEM((NC, XE, YE, 8, 128), f32),
             pltpu.VMEM((2, 4, NT, 8, 128), f32),
             pltpu.VMEM((2, G, 4, 2, 8, 128), f32),

time: 93.8 us -> 80.5 us (0.86)
  Pallas kernels: 73.2 us -> 59.9 us
    pallas_call x1, Pallas kernels: 73.2 us -> 59.9 us  [shards(): pl.pallas_call(kernel, out_shape=jax.ShapeDtypeStruct((2 * NZ * X, G * YB...]
where the time goes in v1:
time: 80.5 us; the launch traced here: 80.2 us
  Pallas kernels  59.9 us (74%)
  starting transfers between devices  10.6 us (13%)
  local copies, waits for them, and re-layouts  7.26 us (9%)
  other arithmetic  2.05 us (3%)
    pallas_call x1, Pallas kernels, shards(): pl.pallas_call(kernel, out_shape=jax.ShapeDtypeStruct((2 * NZ * X, G * YB...  59.9 us
    ppermute x3, starting transfers between devices, neighbours(): return lax.ppermute(value, axis, pairs)  10.6 us
    unnamed x29, local copies, waits for them, and re-layouts  3.3 us
  transfers between devices with their start and end apart: 3, of which 0 were waited for; matrix products, arithmetic and copies ran while one was open for 2% of the time, Pallas kernels for 0%

profile of v1, /device:TPU:57, one launch (start us, length us, event | category | flops | bytes accessed | tf_op | source)
XLA Modules:
  0.0 80.2 jit_solution(11508817033619237676)
XLA Ops:
  0.0 1.4 %copy_convert_fusion = f32[32,8,512]{2,0,1:T(8,128)S(1)} fusion(s32[32,8,512]{2,1,0:T(8,128)} %param.11), kind=kLoop, calls=%fused_computation.3 | loop fusion | flops 131072 | bytes 1048576 | tf_op jit(solution)/shard_map/convert_element_type | solution.py:345
  1.6 4.3 %collective-permute-start = (f32[32,3,32]{2,0,1:T(8,128)S(1)}, f32[32,3,32]{2,0,1:T(8,128)S(1)}, u32[]{:S(2)}, u32[]{:S(2)}) collective-permute-start(f32[32,3,32]{2,0,1:T(8,128)S(1)} %pad_maximum_fusion), channel_id=1, source_target_pairs={{0,16},{16,32},{32,48},{48,64},{64,80},{80,96},{96,112},{1,17},{17... | collective-permute-start | bytes 36872 | tf_op jit(solution)/shard_map/ppermute | solution.py:340
  5.9 1.9 %collective-permute-start.1 = (f32[32,2,32]{2,0,1:T(8,128)S(1)}, f32[32,2,32]{2,0,1:T(8,128)S(1)}, u32[]{:S(2)}, u32[]{:S(2)}) collective-permute-start(f32[32,2,32]{2,0,1:T(8,128)S(1)} %get-tuple-element.11), channel_id=1, source_target_pairs={{16,0},{32,16},{48,32},{64,48},{80,64},{96,80},{112,96},{17,1},{33... | collective-permute-start | bytes 24584 | tf_op jit(solution)/shard_map/ppermute | solution.py:340
  7.9 4.4 %collective-permute-start.2 = (f32[32,8,1]{2,0,1:T(8,128)S(1)}, f32[32,8,1]{2,0,1:T(8,128)S(1)}, u32[]{:S(2)}, u32[]{:S(2)}) collective-permute-start(f32[32,8,1]{2,0,1:T(8,128)S(1)} %slice.53), channel_id=1, source_target_pairs={{0,1},{1,2},{2,3},{3,4},{4,5},{5,6},{6,7},{7,8},{8,9},{9,10},{10,1... | collective-permute-start | bytes 3080 | tf_op jit(solution)/shard_map/ppermute | solution.py:340
  12.5 0.6 copy-done.6
  13.5 0.1 copy.37
  13.6 0.1 stack.41
  13.8 0.2 reshape.44.weights
  13.9 0.5 copy-done.7
  14.7 0.1 multiply_subtract_fusion.1
  15.2 0.1 copy.38
  15.3 0.2 fusion.9
  15.6 0.1 copy.27
  15.7 0.1 stack.33
  15.8 0.1 copy.28
  15.9 0.1 stack.34
  16.1 0.1 copy.29
  16.2 0.1 stack.35
  16.3 0.1 copy.30
  16.5 0.1 stack.36
  16.6 0.1 copy.32
  16.7 0.1 stack.37
  16.9 0.1 copy.33
  17.0 0.1 stack.38
  17.2 0.1 stack.39
  17.5 0.1 stack.40
  17.6 0.1 stack.42
  17.9 0.4 copy.42
  18.4 0.7 copy-done
  19.1 0.2 copy-done.1
  19.3 59.9 %shard_map.91 = f32[512,512]{1,0:T(8,128)S(1)} custom-call(f32[512,512]{1,0:T(8,128)S(1)} %bitcast.17, f32[8,40,512]{2,1,0:T(8,128)S(1)} %pad.48.coef_in, bf16[10,128,128]{2,1,0:T(8,128)(2,1)S(1)} %copy-done.1, f32[128,128]{1,0:T(8,128)S(1)} %reshape.44.weights, bf16[256,128]{1,0:T(8,128)(2,1)S(1)} %copy-done.2, bf16[256,128]{1,0:T(8,128)(2,1)S(1)} %copy-done.3, ...), custom_call_target="tpu_custom_call" | custom-call | tf_op jit(solution)/shard_map/pallas_call | solution.py:390
  79.2 1.0 %copy.63 = f32[2,32,8,512]{3,2,1,0:T(8,128)} copy(f32[2,32,8,512]{3,2,1,0:T(8,128)S(1)} %bitcast.16) | data formatting | bytes 2097152
  (50 shorter events, 1.7 us)
Async XLA Ops:
  0.0 1.4 %copy-start.4 = (f32[3,32,8,32]{3,2,1,0:T(8,128)S(1)}, f32[3,32,8,32]{3,2,1,0:T(8,128)}, u32[]{:S(2)}) copy-start(f32[3,32,8,32]{3,2,1,0:T(8,128)} %param.10) | copy-start | bytes 294916
  1.6 13.1 %collective-permute-start = (f32[32,3,32]{2,0,1:T(8,128)S(1)}, f32[32,3,32]{2,0,1:T(8,128)S(1)}, u32[]{:S(2)}, u32[]{:S(2)}) collective-permute-start(f32[32,3,32]{2,0,1:T(8,128)S(1)} %pad_maximum_fusion), channel_id=1, source_target_pairs={{0,16},{16,32},{32,48},{48,64},{64,80},{80,96},{96,112},{1,17},{17... | collective-permute-start | bytes 36872 | tf_op jit(solution)/shard_map/ppermute | solution.py:340
  5.9 9.0 %collective-permute-start.1 = (f32[32,2,32]{2,0,1:T(8,128)S(1)}, f32[32,2,32]{2,0,1:T(8,128)S(1)}, u32[]{:S(2)}, u32[]{:S(2)}) collective-permute-start(f32[32,2,32]{2,0,1:T(8,128)S(1)} %get-tuple-element.11), channel_id=1, source_target_pairs={{16,0},{32,16},{48,32},{64,48},{80,64},{96,80},{112,96},{17,1},{33... | collective-permute-start | bytes 24584 | tf_op jit(solution)/shard_map/ppermute | solution.py:340
  7.9 7.3 %collective-permute-start.2 = (f32[32,8,1]{2,0,1:T(8,128)S(1)}, f32[32,8,1]{2,0,1:T(8,128)S(1)}, u32[]{:S(2)}, u32[]{:S(2)}) collective-permute-start(f32[32,8,1]{2,0,1:T(8,128)S(1)} %slice.53), channel_id=1, source_target_pairs={{0,1},{1,2},{2,3},{3,4},{4,5},{5,6},{6,7},{7,8},{8,9},{9,10},{10,1... | collective-permute-start | bytes 3080 | tf_op jit(solution)/shard_map/ppermute | solution.py:340
  12.4 1.0 %copy-start.5 = (f32[4,32,4,32]{3,2,1,0:T(4,128)S(1)}, f32[4,32,4,32]{3,2,1,0:T(4,128)}, u32[]{:S(2)}) copy-start(f32[4,32,4,32]{3,2,1,0:T(4,128)} %constant.47) | copy-start | bytes 196612
  12.4 0.8 copy-start.6
  13.7 0.7 copy-start.7
  17.9 1.2 %copy-start = (f32[2,32,8,512]{3,2,1,0:T(8,128)S(1)}, f32[2,32,8,512]{3,2,1,0:T(8,128)}, u32[]{:S(2)}) copy-start(f32[2,32,8,512]{3,2,1,0:T(8,128)} %param.9) | copy-start | bytes 3145732
  18.3 1.1 %copy-start.1 = (bf16[10,128,128]{2,1,0:T(8,128)(2,1)S(1)}, bf16[10,128,128]{2,1,0:T(8,128)(2,1)}, u32[]{:S(2)}) copy-start(bf16[10,128,128]{2,1,0:T(8,128)(2,1)} %constant.23.clone.spread) | copy-start | bytes 983044
  18.3 1.0 %copy-start.2 = (bf16[256,128]{1,0:T(8,128)(2,1)S(1)}, bf16[256,128]{1,0:T(8,128)(2,1)}, u32[]{:S(2)}) copy-start(bf16[256,128]{1,0:T(8,128)(2,1)} %constant.24.clone.own_mat) | copy-start | bytes 196612
  18.3 1.0 %copy-start.3 = (bf16[256,128]{1,0:T(8,128)(2,1)S(1)}, bf16[256,128]{1,0:T(8,128)(2,1)}, u32[]{:S(2)}) copy-start(bf16[256,128]{1,0:T(8,128)(2,1)} %constant.25.clone.past_mat) | copy-start | bytes 196612

commit v2 on v1

--- a/solution.py
+++ b/solution.py
@@ -1,8 +1,5 @@
-import functools
-
 import jax
 import jax.numpy as jnp
-import numpy as np
 from jax import lax
 from jax.experimental import pallas as pl
 from jax.experimental.pallas import tpu as pltpu
@@ -45,8 +42,10 @@
     return b
 
 
-def kernel(tr, coef_in, spread, weights, own_mat, past_mat, mix, out,
-           wmat, tin, tout, sb, rb, fa, fb, adv, edge, coef, so, ro,
+def kernel(tr, velocity, mask, coupling, mixing, out,
+           spread, own_mat, past_mat, mix, wmat, vel, sea3, q, dc, pack_up, pack_down, pack_y, got_low, got_high, got_y,
+           tin, tout, sb, rb, fa, fb, adv, edge, coef, so, ro,
+           statics_in, send_static, recv_static,
            tiles_in, tiles_out, send_in, recv_in, send_halo, recv_x, recv_y, send_out, recv_out, local_sem):
     r, g = lax.axis_index("region"), lax.axis_index("group")
     lane = lax.broadcasted_iota(jnp.int32, (8, 128), 1)
@@ -60,6 +59,14 @@
     def put(j):
         return pltpu.make_async_copy(tout.at[j], out.at[:, pl.ds(j * 128, 128)], tiles_out.at[j])
 
+    at = lax.div(g, 4)
+    spots = (at, jnp.maximum(at - 1, 0), jnp.minimum(at + 1, 3))
+    fetches = [pltpu.make_async_copy(velocity, vel, statics_in.at[0])]
+    for n, spot in enumerate(spots):
+        fetches.append(pltpu.make_async_copy(
+            mask.at[:, :, pl.ds(pl.multiple_of(spot * 128, 128), 128)], sea3.at[n], statics_in.at[n + 1]))
+    for copy in fetches:
+        copy.start()
     for j in range(4):
         fetch(j).start()
 
@@ -85,8 +92,59 @@
     def _():
         pl.semaphore_signal(barrier, inc=1, device_id=(r + 1, g), device_id_type=MESH)
 
+    q[...] = jnp.zeros(q.shape, jnp.float32)
+    for copy in fetches:
+        copy.wait()
+    for k in range(3):
+        q[k, :, 2:10, 2:34] = vel[k]
+    place = lax.rem(g, 4)
+    has_left = jnp.minimum(at, 1).astype(jnp.float32)
+    has_right = jnp.minimum(3 - at, 1).astype(jnp.float32)
+    centre = sea3[0].astype(jnp.float32)
+    left = sea3[1].astype(jnp.float32) * has_left
+    right = sea3[2].astype(jnp.float32) * has_right
+    centre = jnp.where(jnp.logical_and(lane >= 126, place == 0), left, centre)
+    centre = jnp.where(jnp.logical_and(lane < 2, place == 3), right, centre)
+    q[3, :, 2:10, :] = pltpu.roll(centre, lax.rem(130 - 32 * place, 128), 2)
+
+    def level_rows(k, e):
+        return q.at[k].reshape(NZ * 16, 128)[pl.ds(e, NZ, stride=16), :]
+
+    def put_rows(k, e, value):
+        q.at[k].reshape(NZ * 16, 128)[pl.ds(e, NZ, stride=16), :] = value
+
+    pack_up[0], pack_up[1], pack_up[2] = level_rows(3, 8), level_rows(3, 9), level_rows(0, 9)
+    pack_down[0], pack_down[1] = level_rows(3, 2), level_rows(3, 3)
+
+    def pack_level(z, p):
+        return jnp.where(lane == z, pltpu.roll(q[1, z, 2:10, :], lax.rem(z + 95, 128), 1), p)
+
+    pack_y[...] = lax.fori_loop(0, NZ, pack_level, jnp.zeros((8, 128), jnp.float32))
+
     for j in range(4):
         fetch(j).wait()
+
+    def begin(copy):
+        copy.start()
+
+    def static_halo(do):
+        @pl.when(r < R - 1)
+        def _():
+            do(pltpu.make_async_remote_copy(
+                src_ref=pack_up, dst_ref=got_low, send_sem=send_static.at[0], recv_sem=recv_static.at[0],
+                device_id=(r + 1, g), device_id_type=MESH))
+
+        @pl.when(r > 0)
+        def _():
+            do(pltpu.make_async_remote_copy(
+                src_ref=pack_down, dst_ref=got_high, send_sem=send_static.at[1], recv_sem=recv_static.at[1],
+                device_id=(r - 1, g), device_id_type=MESH))
+
+        @pl.when(g < G - 1)
+        def _():
+            do(pltpu.make_async_remote_copy(
+                src_ref=pack_y, dst_ref=got_y, send_sem=send_static.at[2], recv_sem=recv_static.at[2],
+                device_id=(r, g + 1), device_id_type=MESH))
 
     for h, quad in enumerate(QUADS):
         def regroup(n, carry, h=h, quad=quad):
@@ -100,6 +158,7 @@
         lax.fori_loop(0, 8, regroup, 0)
         if h == 0:
             pl.semaphore_wait(barrier, G - 1 + jnp.minimum(r, 1) + jnp.minimum(R - 1 - r, 1))
+            static_halo(begin)
 
         def send(d, carry, h=h):
             to = lax.rem(g + d, G)
@@ -112,23 +171,78 @@
         lax.fori_loop(1, G, send, 0)
         pltpu.make_async_copy(sb.at[g, h], rb.at[h, :, pl.ds(2 * g, 2)], local_sem.at[h]).start()
 
-    high, low = halves(weights[...])
+    def iota(shape, axis):
+        return lax.broadcasted_iota(jnp.int32, shape, axis)
+
+    square = (128, 128)
+    block_in, block_out = iota(square, 0) // 32, iota(square, 1) // 32
+    for k in range(NC):
+        place_k = iota(square, 0) - (4 * k + block_out)
+        hit = jnp.logical_or(place_k == 0, jnp.logical_or(place_k == 4 * NC, place_k == 8 * NC))
+        spread[k] = jnp.where(hit, 1.0, 0.0).astype(jnp.bfloat16)
+    first = iota(square, 0) % 32 == 0
+    own = jnp.where(jnp.logical_and(first, block_in == block_out), 1.0, 0.0).astype(jnp.bfloat16)
+    past = jnp.where(jnp.logical_and(first, block_in < block_out), 1.0, 0.0).astype(jnp.bfloat16)
+    own_mat[...] = jnp.concatenate([own, own], 0)
+    past_mat[...] = jnp.concatenate([past, past], 0)
+    across = jnp.concatenate([coupling[...].T] * 4, 1)
+    weights = jnp.where(block_in == block_out, jnp.concatenate([across] * 4, 0), 0.0)
+    high, low = halves(weights)
     wmat[...] = jnp.concatenate([jnp.concatenate([high, low], 1), jnp.concatenate([high, jnp.zeros_like(low)], 1)], 0)
-
-    def spread_one(zr, carry):
-        d = coef_in[zr]
+    tile = jnp.zeros((8, 128), jnp.float32)
+    for z in range(NZ):
+        tile = jnp.where(jnp.logical_and(row == z % 8, lane // 32 == z // 8), mixing[z], tile)
+    mix[...] = tile
+
+    @pl.when(r > 0)
+    def _():
+        pltpu.make_async_copy(got_low, got_low, recv_static.at[0]).wait()
+        put_rows(3, 0, got_low[0])
+        put_rows(3, 1, got_low[1])
+        put_rows(0, 1, got_low[2])
+
+    @pl.when(r < R - 1)
+    def _():
+        pltpu.make_async_copy(got_high, got_high, recv_static.at[1]).wait()
+        put_rows(3, 10, got_high[0])
+        put_rows(3, 11, got_high[1])
+
+    @pl.when(g > 0)
+    def _():
+        pltpu.make_async_copy(got_y, got_y, recv_static.at[2]).wait()
+
+        def unpack_level(z, carry):
+            q[1, z, 2:10, :] = jnp.where(
+                lane == 1, pltpu.roll(got_y[...], lax.rem(129 - z, 128), 1), q[1, z, 2:10, :])
+            return carry
+
+        lax.fori_loop(0, NZ, unpack_level, 0)
+
+    sea = q[3]
+    follow = (pltpu.roll(sea, 15, 1), pltpu.roll(sea, 127, 2),
+              jnp.concatenate([sea[1:], jnp.zeros((1, 16, 128), jnp.float32)], 0))
+    for k in range(3):
+        opened, c = sea * follow[k], q[k]
+        dc[3 * k] = opened
+        dc[3 * k + 1] = c * opened
+        dc[3 * k + 2] = jnp.where(c > 0, 0.5, -0.5) - 0.5 * c
+    dc[SEA] = sea
+
+    def spread_one(n, carry):
+        e, zr = n // 8, n % 8
+        d = dc.reshape(NC * NZ * 16, 128)[pl.ds(zr * 16 + e, NC * 4, stride=128), :]
         high = d.astype(jnp.bfloat16).astype(jnp.float32)
         rest = d - high
         mid = rest.astype(jnp.bfloat16).astype(jnp.float32)
         low = rest - mid
-        stack = jnp.concatenate([high, mid, low, jnp.zeros((8, 512), jnp.float32)], axis=0)
-        turned = stack.T.astype(jnp.bfloat16)
+        stack = jnp.concatenate([high, mid, low, jnp.zeros((8, 128), jnp.float32)], axis=0)
+        turned = stack.T[:48].astype(jnp.bfloat16)
         for k in range(NC):
             wide = jnp.dot(turned, spread[k], preferred_element_type=jnp.float32)
-            coef.at[k].reshape(XE * YE * 8, 128)[pl.ds(zr, XE * YE, stride=8), :] = wide[:XE * YE]
+            coef.at[k].reshape(XE * YE * 8, 128)[pl.ds(e * YE * 8 + zr, YE, stride=8), :] = wide[:YE]
         return carry
 
-    lax.fori_loop(0, 8, spread_one, 0)
+    lax.fori_loop(0, XE * 8, spread_one, 0)
 
     def x_halo(f, s, do):
         @pl.when(r > 0)
@@ -159,9 +273,6 @@
                 src_ref=f.at[2:10, 32:34], dst_ref=f.at[2:10, 0:2],
                 send_sem=send_halo.at[s, 3], recv_sem=recv_y.at[s, 0],
                 device_id=(r, g + 1), device_id_type=MESH))
-
-    def begin(copy):
-        copy.start()
 
     def arrive(f, s):
         def landed(ref, sem):
@@ -282,6 +393,7 @@
     y_halo(fb, 1, begin)
     arrive(fb, 1)
     advect(fb)
+    static_halo(lambda copy: copy.wait_send())
     for s, f in ((0, fa), (1, fb)):
         x_halo(f, s, lambda copy: copy.wait_send())
         y_halo(f, s, lambda copy: copy.wait_send())
@@ -334,66 +446,32 @@
         put(j).wait()
 
 
-def neighbours(value, axis, shift):
-    size = lax.axis_size(axis)
-    pairs = [(i, i + shift) for i in range(size) if 0 <= i + shift < size]
-    return lax.ppermute(value, axis, pairs)
-
-
-def face_coefficients(velocity, sea_mask, coupling):
-    g = lax.axis_index("group")
-    sea = jnp.pad(sea_mask.astype(jnp.float32), ((0, 0), (0, 0), (2, 2)))
-    sea = lax.dynamic_slice_in_dim(sea, g * YB, YE, axis=2)
-    vx, vy, vz = velocity[0], velocity[1], velocity[2]
-    low = neighbours(jnp.concatenate([sea[:, 6:8, 2:34], vx[:, 7:8]], axis=1), "region", 1)
-    high = neighbours(sea[:, 0:2, 2:34], "region", -1)
-    vy_low = neighbours(vy[:, :, 31:32], "group", 1)
-    edges = ((0, 0), (0, 0), (2, 2))
-    sea = jnp.concatenate([jnp.pad(low[:, 0:2], edges), sea, jnp.pad(high, edges)], axis=1)
-    vx = jnp.pad(jnp.concatenate([low[:, 2:3], vx], axis=1), ((0, 0), (1, 2), (2, 2)))
-    vy = jnp.pad(jnp.concatenate([vy_low, vy], axis=2), ((0, 0), (2, 2), (1, 2)))
-    vz = jnp.pad(vz, ((0, 0), (2, 2), (2, 2)))
-    ends = [(0, 0)] * 3
-    parts = []
-    for axis, c in ((1, vx), (2, vy), (0, vz)):
-        pad = [(0, 1) if n == axis else (0, 0) for n in range(3)]
-        following = jnp.pad(lax.slice_in_dim(sea, 1, sea.shape[axis], axis=axis), pad)
-        opened = sea * following
-        parts += [opened, c * opened, 0.5 * jnp.sign(c) - 0.5 * c]
-    parts.append(sea)
-    whole = jnp.stack(parts, 0).reshape(NC, 4, 8, XE * YE)
-    whole = jnp.moveaxis(whole, 2, 0).reshape(8, NC * 4, XE * YE)
-    return jnp.pad(whole, ((0, 0), (0, 0), (0, 512 - XE * YE)))
-
-
 def shards(tracers, velocity, sea_mask, coupling, mixing):
-    coef_in = face_coefficients(velocity, sea_mask, coupling)
-    spread = np.zeros((NC, 3, NC, 4, 4, NT), np.float32)
-    for k in range(NC):
-        for b in range(4):
-            spread[k, :, k, b, b] = 1
-    spread = np.pad(spread.reshape(NC, 3 * NC * 4, 128), ((0, 0), (0, 8), (0, 0)))
-    own = np.zeros((4, NT, 4, NT), np.float32)
-    past = np.zeros((4, NT, 4, NT), np.float32)
-    for a in range(4):
-        own[a, 0, a] = 1
-        past[a, 0, a + 1:] = 1
-    own, past = own.reshape(128, 128), past.reshape(128, 128)
-    own, past = np.concatenate([own, own], 0), np.concatenate([past, past], 0)
-    block = np.kron(np.eye(4, dtype=np.float32), np.ones((NT, NT), np.float32))
-    weights = jnp.tile(coupling.T, (4, 4)) * block
-    mix = jnp.broadcast_to(mixing.reshape(4, 8).T[:, :, None], (8, 4, NT)).reshape(8, 128)
-
+    anywhere = pl.BlockSpec(memory_space=pl.ANY)
     vmem = pl.BlockSpec(memory_space=pltpu.VMEM)
     f32 = jnp.float32
     dma = pltpu.SemaphoreType.DMA
     out = pl.pallas_call(
         kernel,
         out_shape=jax.ShapeDtypeStruct((2 * NZ * X, G * YB), f32),
-        in_specs=[pl.BlockSpec(memory_space=pl.ANY)] + [vmem] * 6,
-        out_specs=pl.BlockSpec(memory_space=pl.ANY),
+        in_specs=[anywhere] * 3 + [vmem, pl.BlockSpec(memory_space=pltpu.SMEM)],
+        out_specs=anywhere,
         scratch_shapes=[
+            pltpu.VMEM((NC, 128, 128), jnp.bfloat16),
+            pltpu.VMEM((256, 128), jnp.bfloat16),
+            pltpu.VMEM((256, 128), jnp.bfloat16),
+            pltpu.VMEM((8, 128), f32),
             pltpu.VMEM((256, 256), jnp.bfloat16),
+            pltpu.VMEM((3, NZ, X, YB), f32),
+            pltpu.VMEM((3, NZ, X, 128), jnp.int32),
+            pltpu.VMEM((4, NZ, 16, 128), f32),
+            pltpu.VMEM((NC, NZ, 16, 128), f32),
+            pltpu.VMEM((3, NZ, 128), f32),
+            pltpu.VMEM((2, NZ, 128), f32),
+            pltpu.VMEM((8, 128), f32),
+            pltpu.VMEM((3, NZ, 128), f32),
+            pltpu.VMEM((2, NZ, 128), f32),
+            pltpu.VMEM((8, 128), f32),
             pltpu.VMEM((4, 2 * NZ * X, 128), f32),
             pltpu.VMEM((4, 2 * NZ * X, 128), f32),
             pltpu.VMEM((G, 2, 4, 2, 8, 128), f32),
@@ -405,13 +483,12 @@
             pltpu.VMEM((NC, XE, YE, 8, 128), f32),
             pltpu.VMEM((2, 4, NT, 8, 128), f32),
             pltpu.VMEM((2, G, 4, 2, 8, 128), f32),
+            dma((4,)), dma((3,)), dma((3,)),
             dma((4,)), dma((4,)), dma((2,)), dma((2,)), dma((2, 4)), dma((2, 2)), dma((2, 2)), dma((2,)), dma((2,)), dma((4,)),
         ],
         compiler_params=pltpu.CompilerParams(
             collective_id=0, has_side_effects=True, vmem_limit_bytes=48 * 2**20),
-    )(tracers.reshape(2 * NZ * X, G * YB), coef_in,
-      jnp.asarray(spread, jnp.bfloat16), weights, jnp.asarray(own, jnp.bfloat16),
-      jnp.asarray(past, jnp.bfloat16), mix)
+    )(tracers.reshape(2 * NZ * X, G * YB), velocity, sea_mask, coupling, mixing)
     return out.reshape(tracers.shape)
 
 

time: 80.5 us -> 89.2 us (1.11)
  Pallas kernels: 59.9 us -> 82.7 us
  starting transfers between devices: 10.6 us -> 0 us
  other arithmetic: 2.05 us -> 0 us
  local copies, waits for them, and re-layouts: 7.26 us -> 5.6 us
    pallas_call x1, Pallas kernels: 59.9 us -> 82.7 us  [shards(): pl.pallas_call(kernel, out_shape=jax.ShapeDtypeStruct((2 * NZ * X, G * YB...]
    ppermute x3 -> x0, starting transfers between devices: 10.6 us -> none  [neighbours(): return lax.ppermute(value, axis, pairs)]
    unnamed x29 -> x11, local copies, waits for them, and re-layouts: 3.3 us -> 5.6 us
    convert_element_type x1 -> x0, other arithmetic: 1.4 us -> none  [face_coefficients(): sea = jnp.pad(sea_mask.astype(jnp.float32), ((0, 0), (0, 0), (2, 2)))]
    another operation x11 -> x0, local copies, waits for them, and re-layouts: 1.3 us -> none  [face_coefficients(): whole = jnp.stack(parts, 0).reshape(NC, 4, 8, XE * YE)]
  transfers between devices with their start and end apart: 3 -> 0, of which waited for: 0 -> 0; matrix products, arithmetic and copies ran while one was open for 2% -> 0% of each run, Pallas kernels for 0% -> 0%
where the time goes in v2:
time: 89.2 us; the launch traced here: 88.3 us
  Pallas kernels  82.7 us (93%)
  local copies, waits for them, and re-layouts  5.6 us (6%)
    pallas_call x1, Pallas kernels, shards(): pl.pallas_call(kernel, out_shape=jax.ShapeDtypeStruct((2 * NZ * X, G * YB...  82.7 us
    unnamed x11, local copies, waits for them, and re-layouts  5.6 us

profile of v2, /device:TPU:57, one launch (start us, length us, event | category | flops | bytes accessed | tf_op | source)
XLA Modules:
  0.0 88.3 jit_solution(17456946088290509092)
XLA Ops:
  0.0 0.0 copy-start.4
  0.0 0.7 copy-done.4
  0.7 0.0 copy-start
  0.7 1.2 %copy-done = f32[2,32,8,512]{3,2,1,0:T(8,128)S(1)} copy-done((f32[2,32,8,512]{3,2,1,0:T(8,128)S(1)}, f32[2,32,8,512]{3,2,1,0:T(8,128)}, u32[]{:S(2)}) %copy-start) | copy-done | bytes 1048600
  1.9 0.0 copy-start.1
  1.9 1.0 %copy-done.1 = s32[32,8,512]{2,1,0:T(8,128)S(1)} copy-done((s32[32,8,512]{2,1,0:T(8,128)S(1)}, s32[32,8,512]{2,1,0:T(8,128)}, u32[]{:S(2)}) %copy-start.1) | copy-done | bytes 524312
  2.9 0.0 copy-start.2
  2.9 1.0 %copy-done.2 = f32[3,32,8,32]{3,2,1,0:T(8,128)S(1)} copy-done((f32[3,32,8,32]{3,2,1,0:T(8,128)S(1)}, f32[3,32,8,32]{3,2,1,0:T(8,128)}, u32[]{:S(2)}) %copy-start.2) | copy-done | bytes 98328
  3.9 0.0 copy-start.3
  3.9 0.7 copy-done.3
  4.6 82.7 %shard_map.55 = f32[512,512]{1,0:T(8,128)S(1)} custom-call(f32[512,512]{1,0:T(8,128)S(1)} %bitcast.3, f32[3,32,8,32]{3,2,1,0:T(8,128)S(1)} %copy-done.2, s32[32,8,512]{2,1,0:T(8,128)S(1)} %copy-done.1, f32[32,32]{1,0:T(8,128)S(1)} %copy-done.3, f32[32]{0:T(128)S(1)} %copy-done.4), custom_call_target="tpu_custom_call" | custom-call | tf_op jit(solution)/shard_map/pallas_call | solution.py:454
  87.4 1.0 %copy.7 = f32[2,32,8,512]{3,2,1,0:T(8,128)} copy(f32[2,32,8,512]{3,2,1,0:T(8,128)S(1)} %bitcast.2) | data formatting | bytes 2097152
Async XLA Ops:
  0.0 0.7 copy-start.4
  0.7 1.2 %copy-start = (f32[2,32,8,512]{3,2,1,0:T(8,128)S(1)}, f32[2,32,8,512]{3,2,1,0:T(8,128)}, u32[]{:S(2)}) copy-start(f32[2,32,8,512]{3,2,1,0:T(8,128)} %param.5) | copy-start | bytes 3145732
  1.9 1.0 %copy-start.1 = (s32[32,8,512]{2,1,0:T(8,128)S(1)}, s32[32,8,512]{2,1,0:T(8,128)}, u32[]{:S(2)}) copy-start(s32[32,8,512]{2,1,0:T(8,128)} %mask.1) | copy-start | bytes 1572868
  2.9 1.0 %copy-start.2 = (f32[3,32,8,32]{3,2,1,0:T(8,128)S(1)}, f32[3,32,8,32]{3,2,1,0:T(8,128)}, u32[]{:S(2)}) copy-start(f32[3,32,8,32]{3,2,1,0:T(8,128)} %velocity.1) | copy-start | bytes 294916
  3.9 0.7 copy-start.3

commit v3 on v2

--- a/solution.py
+++ b/solution.py
@@ -10,16 +10,17 @@
 NZ, NT, X, YB, G, R = 32, 32, 8, 32, 16, 8
 XE, YE = X + 4, YB + 4
 QUADS = ((0, 1, 6, 7), (2, 3, 4, 5))
-NC = 10
-OX, CX, QX, OY, CY, QY, OZ, CZ, QZ, SEA = range(NC)
+NC = 5
+CX, CY, CZ, SEA, OZ = range(NC)
 
 
 def minmod(a, b):
     return jnp.maximum(jnp.minimum(a, b), jnp.minimum(jnp.maximum(a, b), 0.0))
 
 
-def face(cell, following, slope, slope_following, c, q):
+def face(cell, following, slope, slope_following, c):
     forward = c > 0
+    q = jnp.where(forward, 0.5, -0.5) - 0.5 * c
     return c * (jnp.where(forward, cell, following) + q * jnp.where(forward, slope, slope_following))
 
 
@@ -43,7 +44,7 @@
 
 
 def kernel(tr, velocity, mask, coupling, mixing, out,
-           spread, own_mat, past_mat, mix, wmat, vel, sea3, q, dc, pack_up, pack_down, pack_y, got_low, got_high, got_y,
+           spread, stacked, own_mat, past_mat, mix, wmat, vel, sea3, q, dc, pack_up, pack_down, pack_y, got_low, got_high, got_y,
            tin, tout, sb, rb, fa, fb, adv, edge, coef, so, ro,
            statics_in, send_static, recv_static,
            tiles_in, tiles_out, send_in, recv_in, send_halo, recv_x, recv_y, send_out, recv_out, local_sem):
@@ -176,10 +177,12 @@
 
     square = (128, 128)
     block_in, block_out = iota(square, 0) // 32, iota(square, 1) // 32
-    for k in range(NC):
-        place_k = iota(square, 0) - (4 * k + block_out)
-        hit = jnp.logical_or(place_k == 0, jnp.logical_or(place_k == 4 * NC, place_k == 8 * NC))
-        spread[k] = jnp.where(hit, 1.0, 0.0).astype(jnp.bfloat16)
+    for level in range(4):
+        for k in range(NC):
+            base = 32 * level + (24 + 4 * (k - 3) if k >= 3 else 4 * k)
+            place_k = iota(square, 0) - (base + block_out)
+            hit = place_k == 0 if k >= 3 else jnp.logical_or(place_k == 0, place_k == 12)
+            spread[level, k] = jnp.where(hit, 1.0, 0.0).astype(jnp.bfloat16)
     first = iota(square, 0) % 32 == 0
     own = jnp.where(jnp.logical_and(first, block_in == block_out), 1.0, 0.0).astype(jnp.bfloat16)
     past = jnp.where(jnp.logical_and(first, block_in < block_out), 1.0, 0.0).astype(jnp.bfloat16)
@@ -222,27 +225,31 @@
     follow = (pltpu.roll(sea, 15, 1), pltpu.roll(sea, 127, 2),
               jnp.concatenate([sea[1:], jnp.zeros((1, 16, 128), jnp.float32)], 0))
     for k in range(3):
-        opened, c = sea * follow[k], q[k]
-        dc[3 * k] = opened
-        dc[3 * k + 1] = c * opened
-        dc[3 * k + 2] = jnp.where(c > 0, 0.5, -0.5) - 0.5 * c
-    dc[SEA] = sea
-
-    def spread_one(n, carry):
-        e, zr = n // 8, n % 8
-        d = dc.reshape(NC * NZ * 16, 128)[pl.ds(zr * 16 + e, NC * 4, stride=128), :]
-        high = d.astype(jnp.bfloat16).astype(jnp.float32)
-        rest = d - high
-        mid = rest.astype(jnp.bfloat16).astype(jnp.float32)
-        low = rest - mid
-        stack = jnp.concatenate([high, mid, low, jnp.zeros((8, 128), jnp.float32)], axis=0)
-        turned = stack.T[:48].astype(jnp.bfloat16)
+        opened = sea * follow[k]
+        c = q[k] * opened
+        high = c.astype(jnp.bfloat16).astype(jnp.float32)
+        dc[k] = high
+        dc[3 + k] = c - high
+    dc[6] = sea
+    dc[7] = opened
+
+    def stack_one(e, carry):
+        for half in range(2):
+            rows = [dc.reshape(8 * NZ * 16, 128)[pl.ds((half * 4 + n) * 16 + e, 32, stride=128), :] for n in range(4)]
+            stacked[half, pl.ds(pl.multiple_of(e * 48, 16), 48), :] = (
+                jnp.concatenate(rows, axis=0).T[:48].astype(jnp.bfloat16))
+        return carry
+
+    lax.fori_loop(0, XE, stack_one, 0)
+
+    def spread_one(zr, carry):
         for k in range(NC):
-            wide = jnp.dot(turned, spread[k], preferred_element_type=jnp.float32)
-            coef.at[k].reshape(XE * YE * 8, 128)[pl.ds(e * YE * 8 + zr, YE, stride=8), :] = wide[:YE]
+            wide = jnp.dot(stacked[zr // 4], spread[zr % 4, k], preferred_element_type=jnp.float32)
+            for e in range(XE):
+                coef.at[k].reshape(XE * YE * 8, 128)[pl.ds(e * YE * 8 + zr, YE, stride=8), :] = wide[e * 48:e * 48 + YE]
         return carry
 
-    lax.fori_loop(0, XE * 8, spread_one, 0)
+    lax.fori_loop(0, 8, spread_one, 0)
 
     def x_halo(f, s, do):
         @pl.when(r > 0)
@@ -323,7 +330,7 @@
         jump = (next0 - last) * static(OZ, 7)
         slope = minmod((last - rows(f, 6)) * static(OZ, 6), jump)
         slope_next = minmod(jump, (next1 - next0) * pltpu.roll(static(OZ, 0), 96, 1))
-        flux = face(last, next0, slope, slope_next, static(CZ, 7), static(QZ, 7)) - mix[7:8, :] * jump
+        flux = face(last, next0, slope, slope_next, static(CZ, 7)) - mix[7:8, :] * jump
         for n, k, v in ((0, 7, next0), (0, 0, pltpu.roll(jump, 32, 1)), (1, 7, slope_next), (1, 0, pltpu.roll(flux, 32, 1))):
             edge.at[n].reshape(X * YE * 8, 128)[pl.ds(k, X * YE, stride=8), :] = v
 
@@ -337,31 +344,35 @@
             return coef[k, 2:10, e]
 
         f1, f2 = cells(1), cells(2)
-        j0 = (f1 - cells(0)) * along(OY, 0)
-        j1 = (f2 - f1) * along(OY, 1)
-        j2 = (cells(3) - f2) * along(OY, 2)
+        def open_y(e):
+            return along(SEA, e) * along(SEA, e + 1)
+
+        j0 = (f1 - cells(0)) * open_y(0)
+        j1 = (f2 - f1) * open_y(1)
+        j2 = (cells(3) - f2) * open_y(2)
         s1, s2 = minmod(j0, j1), minmod(j1, j2)
-        start = (j2, s2, face(f1, f2, s1, s2, along(CY, 1), along(QY, 1)))
+        start = (j2, s2, face(f1, f2, s1, s2, along(CY, 1)))
 
         def column(y, carry):
             jump, slope, before = carry
             e = y + 2
             fx = f[:, e]
             inner, following = fx[2:10], cells(e + 1)
-            jump_next = (cells(e + 2) - following) * along(OY, e + 1)
+            jump_next = (cells(e + 2) - following) * open_y(e + 1)
             slope_next = minmod(jump, jump_next)
-            after = face(inner, following, slope, slope_next, along(CY, e), along(QY, e))
+            after = face(inner, following, slope, slope_next, along(CY, e))
             total = inner - (after - before)
-            jx = (fx[1:] - fx[:-1]) * coef[OX, 0:11, e]
+            sea_x = coef[SEA, :, e]
+            jx = (fx[1:] - fx[:-1]) * (sea_x[1:] * sea_x[:-1])
             sx = minmod(jx[:-1], jx[1:])
-            flux = face(fx[1:10], fx[2:11], sx[:-1], sx[1:], coef[CX, 1:10, e], coef[QX, 1:10, e])
+            flux = face(fx[1:10], fx[2:11], sx[:-1], sx[1:], coef[CX, 1:10, e])
             total = total - (flux[1:] - flux[:-1])
             edge0, edge1 = edge[0, :, e], edge[1, :, e]
             below = jnp.where(row == 7, edge0, pltpu.roll(inner, 7, 1))
             jz = (below - inner) * along(OZ, e)
             sz = minmod(jnp.where(row == 0, edge0, pltpu.roll(jz, 1, 1)), jz)
             sz_next = jnp.where(row == 7, edge1, pltpu.roll(sz, 7, 1))
-            down = face(inner, below, sz, sz_next, along(CZ, e), along(QZ, e)) - mix[...] * jz
+            down = face(inner, below, sz, sz_next, along(CZ, e)) - mix[...] * jz
             adv[:, y] = total - (down - jnp.where(row == 0, edge1, pltpu.roll(down, 1, 1)))
             return jump_next, slope_next, after
 
@@ -457,7 +468,8 @@
         in_specs=[anywhere] * 3 + [vmem, pl.BlockSpec(memory_space=pltpu.SMEM)],
         out_specs=anywhere,
         scratch_shapes=[
-            pltpu.VMEM((NC, 128, 128), jnp.bfloat16),
+            pltpu.VMEM((4, NC, 128, 128), jnp.bfloat16),
+            pltpu.VMEM((2, XE * 48, 128), jnp.bfloat16),
             pltpu.VMEM((256, 128), jnp.bfloat16),
             pltpu.VMEM((256, 128), jnp.bfloat16),
             pltpu.VMEM((8, 128), f32),
@@ -465,7 +477,7 @@
             pltpu.VMEM((3, NZ, X, YB), f32),
             pltpu.VMEM((3, NZ, X, 128), jnp.int32),
             pltpu.VMEM((4, NZ, 16, 128), f32),
-            pltpu.VMEM((NC, NZ, 16, 128), f32),
+            pltpu.VMEM((8, NZ, 16, 128), f32),
             pltpu.VMEM((3, NZ, 128), f32),
             pltpu.VMEM((2, NZ, 128), f32),
             pltpu.VMEM((8, 128), f32),

time: 89.2 us -> 68.3 us (0.77)
  the two profiles are of different devices: /device:TPU:57 before, /device:TPU:37 now
where the time goes in v3:
time: 68.3 us; the launch traced here: 68 us
  Pallas kernels  62.4 us (91%)
  local copies, waits for them, and re-layouts  5.6 us (8%)
    pallas_call x1, Pallas kernels, shards(): pl.pallas_call(kernel, out_shape=jax.ShapeDtypeStruct((2 * NZ * X, G * YB...  62.4 us
    unnamed x11, local copies, waits for them, and re-layouts  5.6 us

profile of v3, /device:TPU:37, one launch (start us, length us, event | category | flops | bytes accessed | tf_op | source)
XLA Modules:
  0.0 68.0 jit_solution(12969750114540174105)
XLA Ops:
  0.0 0.0 copy-start.4
  0.0 0.7 copy-done.4
  0.7 0.0 copy-start
  0.7 1.2 %copy-done = f32[2,32,8,512]{3,2,1,0:T(8,128)S(1)} copy-done((f32[2,32,8,512]{3,2,1,0:T(8,128)S(1)}, f32[2,32,8,512]{3,2,1,0:T(8,128)}, u32[]{:S(2)}) %copy-start) | copy-done | bytes 1048600
  1.9 0.0 copy-start.1
  1.9 1.0 %copy-done.1 = s32[32,8,512]{2,1,0:T(8,128)S(1)} copy-done((s32[32,8,512]{2,1,0:T(8,128)S(1)}, s32[32,8,512]{2,1,0:T(8,128)}, u32[]{:S(2)}) %copy-start.1) | copy-done | bytes 524312
  2.9 0.0 copy-start.2
  2.9 1.0 %copy-done.2 = f32[3,32,8,32]{3,2,1,0:T(8,128)S(1)} copy-done((f32[3,32,8,32]{3,2,1,0:T(8,128)S(1)}, f32[3,32,8,32]{3,2,1,0:T(8,128)}, u32[]{:S(2)}) %copy-start.2) | copy-done | bytes 98328
  3.9 0.0 copy-start.3
  3.9 0.7 %copy-done.3 = f32[32,32]{1,0:T(8,128)S(1)} copy-done((f32[32,32]{1,0:T(8,128)S(1)}, f32[32,32]{1,0:T(8,128)}, u32[]{:S(2)}) %copy-start.3) | copy-done | bytes 4120
  4.6 62.4 %shard_map.55 = f32[512,512]{1,0:T(8,128)S(1)} custom-call(f32[512,512]{1,0:T(8,128)S(1)} %bitcast.3, f32[3,32,8,32]{3,2,1,0:T(8,128)S(1)} %copy-done.2, s32[32,8,512]{2,1,0:T(8,128)S(1)} %copy-done.1, f32[32,32]{1,0:T(8,128)S(1)} %copy-done.3, f32[32]{0:T(128)S(1)} %copy-done.4), custom_call_target="tpu_custom_call" | custom-call | tf_op jit(solution)/shard_map/pallas_call | solution.py:465
  67.0 1.0 %copy.7 = f32[2,32,8,512]{3,2,1,0:T(8,128)} copy(f32[2,32,8,512]{3,2,1,0:T(8,128)S(1)} %bitcast.2) | data formatting | bytes 2097152
Async XLA Ops:
  0.0 0.7 copy-start.4
  0.7 1.2 %copy-start = (f32[2,32,8,512]{3,2,1,0:T(8,128)S(1)}, f32[2,32,8,512]{3,2,1,0:T(8,128)}, u32[]{:S(2)}) copy-start(f32[2,32,8,512]{3,2,1,0:T(8,128)} %param.5) | copy-start | bytes 3145732
  1.9 1.0 %copy-start.1 = (s32[32,8,512]{2,1,0:T(8,128)S(1)}, s32[32,8,512]{2,1,0:T(8,128)}, u32[]{:S(2)}) copy-start(s32[32,8,512]{2,1,0:T(8,128)} %mask.1) | copy-start | bytes 1572868
  2.9 1.0 %copy-start.2 = (f32[3,32,8,32]{3,2,1,0:T(8,128)S(1)}, f32[3,32,8,32]{3,2,1,0:T(8,128)}, u32[]{:S(2)}) copy-start(f32[3,32,8,32]{3,2,1,0:T(8,128)} %velocity.1) | copy-start | bytes 294916
  3.9 0.7 %copy-start.3 = (f32[32,32]{1,0:T(8,128)S(1)}, f32[32,32]{1,0:T(8,128)}, u32[]{:S(2)}) copy-start(f32[32,32]{1,0:T(8,128)} %coupling.1) | copy-start | bytes 12292

commit v4 on v3

--- a/solution.py
+++ b/solution.py
@@ -10,6 +10,7 @@
 NZ, NT, X, YB, G, R = 32, 32, 8, 32, 16, 8
 XE, YE = X + 4, YB + 4
 QUADS = ((0, 1, 6, 7), (2, 3, 4, 5))
+RANGES = (((0, 2), (6, 8)), ((2, 6),))
 NC = 5
 CX, CY, CZ, SEA, OZ = range(NC)
 
@@ -43,11 +44,11 @@
     return b
 
 
-def kernel(tr, velocity, mask, coupling, mixing, out,
-           spread, stacked, own_mat, past_mat, mix, wmat, vel, sea3, q, dc, pack_up, pack_down, pack_y, got_low, got_high, got_y,
-           tin, tout, sb, rb, fa, fb, adv, edge, coef, so, ro,
+def kernel(tr, velocity, mask, coupling_in, mixing_in, out,
+           coupling, mixing, spread, stacked, own_mat, past_mat, mix, wmat, vel, sea3, q, dc, pack_up, pack_down, pack_y, got_low, got_high, got_y,
+           tin, tout, sb, rb, fa, fb, fc, adv, edge, coef, so, ro,
            statics_in, send_static, recv_static,
-           tiles_in, tiles_out, send_in, recv_in, send_halo, recv_x, recv_y, send_out, recv_out, local_sem):
+           tiles_in, tiles_out, send_in, recv_in, send_halo, recv_x, send_y, recv_y, send_out, recv_out, local_sem):
     r, g = lax.axis_index("region"), lax.axis_index("group")
     lane = lax.broadcasted_iota(jnp.int32, (8, 128), 1)
     row = lax.broadcasted_iota(jnp.int32, (8, 128), 0)
@@ -62,7 +63,9 @@
 
     at = lax.div(g, 4)
     spots = (at, jnp.maximum(at - 1, 0), jnp.minimum(at + 1, 3))
-    fetches = [pltpu.make_async_copy(velocity, vel, statics_in.at[0])]
+    fetches = [pltpu.make_async_copy(velocity, vel, statics_in.at[0]),
+               pltpu.make_async_copy(coupling_in, coupling, statics_in.at[4]),
+               pltpu.make_async_copy(mixing_in, mixing, statics_in.at[5])]
     for n, spot in enumerate(spots):
         fetches.append(pltpu.make_async_copy(
             mask.at[:, :, pl.ds(pl.multiple_of(spot * 128, 128), 128)], sea3.at[n], statics_in.at[n + 1]))
@@ -92,6 +95,55 @@
     @pl.when(r < R - 1)
     def _():
         pl.semaphore_signal(barrier, inc=1, device_id=(r + 1, g), device_id_type=MESH)
+
+    for j in range(4):
+        fetch(j).wait()
+
+    def begin(copy):
+        copy.start()
+
+    def static_halo(do):
+        @pl.when(r < R - 1)
+        def _():
+            do(pltpu.make_async_remote_copy(
+                src_ref=pack_up, dst_ref=got_low, send_sem=send_static.at[0], recv_sem=recv_static.at[0],
+                device_id=(r + 1, g), device_id_type=MESH))
+
+        @pl.when(r > 0)
+        def _():
+            do(pltpu.make_async_remote_copy(
+                src_ref=pack_down, dst_ref=got_high, send_sem=send_static.at[1], recv_sem=recv_static.at[1],
+                device_id=(r - 1, g), device_id_type=MESH))
+
+        @pl.when(g < G - 1)
+        def _():
+            do(pltpu.make_async_remote_copy(
+                src_ref=pack_y, dst_ref=got_y, send_sem=send_static.at[2], recv_sem=recv_static.at[2],
+                device_id=(r, g + 1), device_id_type=MESH))
+
+    for h, quad in enumerate(QUADS):
+        def regroup(n, carry, h=h, quad=quad):
+            t, zq = n // 4, n % 4
+            for j in range(4):
+                v = [tin[j, pl.ds((t * NZ + zq * 8) * X + x, 8, stride=8), :] for x in quad]
+                for i, b in enumerate(block_swap(v, lane)):
+                    sb[4 * j + i, h, zq, t] = b
+            return carry
+
+        lax.fori_loop(0, 8, regroup, 0, unroll=4)
+        if h == 0:
+            pl.semaphore_wait(barrier, G - 1 + jnp.minimum(r, 1) + jnp.minimum(R - 1 - r, 1))
+
+        def send(d, carry, h=h):
+            to = lax.rem(g + d, G)
+            pltpu.make_async_remote_copy(
+                src_ref=sb.at[to, h], dst_ref=rb.at[h, :, pl.ds(2 * g, 2)],
+                send_sem=send_in.at[h], recv_sem=recv_in.at[h],
+                device_id=(r, to), device_id_type=MESH).start()
+            return carry
+
+        lax.fori_loop(1, G, send, 0)
+        pltpu.make_async_copy(sb.at[g, h], rb.at[h, :, pl.ds(2 * g, 2)], local_sem.at[h]).start()
 
     q[...] = jnp.zeros(q.shape, jnp.float32)
     for copy in fetches:
@@ -120,57 +172,9 @@
     def pack_level(z, p):
         return jnp.where(lane == z, pltpu.roll(q[1, z, 2:10, :], lax.rem(z + 95, 128), 1), p)
 
-    pack_y[...] = lax.fori_loop(0, NZ, pack_level, jnp.zeros((8, 128), jnp.float32))
-
-    for j in range(4):
-        fetch(j).wait()
-
-    def begin(copy):
-        copy.start()
-
-    def static_halo(do):
-        @pl.when(r < R - 1)
-        def _():
-            do(pltpu.make_async_remote_copy(
-                src_ref=pack_up, dst_ref=got_low, send_sem=send_static.at[0], recv_sem=recv_static.at[0],
-                device_id=(r + 1, g), device_id_type=MESH))
-
-        @pl.when(r > 0)
-        def _():
-            do(pltpu.make_async_remote_copy(
-                src_ref=pack_down, dst_ref=got_high, send_sem=send_static.at[1], recv_sem=recv_static.at[1],
-                device_id=(r - 1, g), device_id_type=MESH))
-
-        @pl.when(g < G - 1)
-        def _():
-            do(pltpu.make_async_remote_copy(
-                src_ref=pack_y, dst_ref=got_y, send_sem=send_static.at[2], recv_sem=recv_static.at[2],
-                device_id=(r, g + 1), device_id_type=MESH))
-
-    for h, quad in enumerate(QUADS):
-        def regroup(n, carry, h=h, quad=quad):
-            t, zq = n // 4, n % 4
-            for j in range(4):
-                v = [tin[j, pl.ds((t * NZ + zq * 8) * X + x, 8, stride=8), :] for x in quad]
-                for i, b in enumerate(block_swap(v, lane)):
-                    sb[4 * j + i, h, zq, t] = b
-            return carry
-
-        lax.fori_loop(0, 8, regroup, 0)
-        if h == 0:
-            pl.semaphore_wait(barrier, G - 1 + jnp.minimum(r, 1) + jnp.minimum(R - 1 - r, 1))
-            static_halo(begin)
-
-        def send(d, carry, h=h):
-            to = lax.rem(g + d, G)
-            pltpu.make_async_remote_copy(
-                src_ref=sb.at[to, h], dst_ref=rb.at[h, :, pl.ds(2 * g, 2)],
-                send_sem=send_in.at[h], recv_sem=recv_in.at[h],
-                device_id=(r, to), device_id_type=MESH).start()
-            return carry
-
-        lax.fori_loop(1, G, send, 0)
-        pltpu.make_async_copy(sb.at[g, h], rb.at[h, :, pl.ds(2 * g, 2)], local_sem.at[h]).start()
+    pack_y[...] = lax.fori_loop(0, NZ, pack_level, jnp.zeros((8, 128), jnp.float32), unroll=8)
+
+    static_halo(begin)
 
     def iota(shape, axis):
         return lax.broadcasted_iota(jnp.int32, shape, axis)
@@ -219,7 +223,7 @@
                 lane == 1, pltpu.roll(got_y[...], lax.rem(129 - z, 128), 1), q[1, z, 2:10, :])
             return carry
 
-        lax.fori_loop(0, NZ, unpack_level, 0)
+        lax.fori_loop(0, NZ, unpack_level, 0, unroll=8)
 
     sea = q[3]
     follow = (pltpu.roll(sea, 15, 1), pltpu.roll(sea, 127, 2),
@@ -266,25 +270,27 @@
                 send_sem=send_halo.at[s, 1], recv_sem=recv_x.at[s, 0],
                 device_id=(r + 1, g), device_id_type=MESH))
 
-    def y_halo(f, s, do):
+    def y_halo(f, s, h):
         @pl.when(g > 0)
         def _():
-            do(pltpu.make_async_remote_copy(
-                src_ref=f.at[2:10, 2:4], dst_ref=f.at[2:10, 34:36],
-                send_sem=send_halo.at[s, 2], recv_sem=recv_y.at[s, 1],
-                device_id=(r, g - 1), device_id_type=MESH))
+            for x0, x1 in RANGES[h]:
+                pltpu.make_async_remote_copy(
+                    src_ref=f.at[x0 + 2:x1 + 2, 2:4], dst_ref=f.at[x0 + 2:x1 + 2, 34:36],
+                    send_sem=send_y.at[s, h, 1], recv_sem=recv_y.at[s, h, 1],
+                    device_id=(r, g - 1), device_id_type=MESH).start()
 
         @pl.when(g < G - 1)
         def _():
-            do(pltpu.make_async_remote_copy(
-                src_ref=f.at[2:10, 32:34], dst_ref=f.at[2:10, 0:2],
-                send_sem=send_halo.at[s, 3], recv_sem=recv_y.at[s, 0],
-                device_id=(r, g + 1), device_id_type=MESH))
-
-    def arrive(f, s):
-        def landed(ref, sem):
-            pltpu.make_async_copy(ref, ref, sem).wait()
-
+            for x0, x1 in RANGES[h]:
+                pltpu.make_async_remote_copy(
+                    src_ref=f.at[x0 + 2:x1 + 2, 32:34], dst_ref=f.at[x0 + 2:x1 + 2, 0:2],
+                    send_sem=send_y.at[s, h, 0], recv_sem=recv_y.at[s, h, 0],
+                    device_id=(r, g + 1), device_id_type=MESH).start()
+
+    def landed(ref, sem):
+        pltpu.make_async_copy(ref, ref, sem).wait()
+
+    def arrive_x(f, s):
         @pl.when(r > 0)
         def _():
             landed(f.at[0:2, 2:34], recv_x.at[s, 0])
@@ -293,13 +299,23 @@
         def _():
             landed(f.at[10:12, 2:34], recv_x.at[s, 1])
 
+    def arrive_y(f, s, h):
         @pl.when(g > 0)
         def _():
-            landed(f.at[2:10, 0:2], recv_y.at[s, 0])
+            landed(f.at[2:6, 0:2], recv_y.at[s, h, 0])
 
         @pl.when(g < G - 1)
         def _():
-            landed(f.at[2:10, 34:36], recv_y.at[s, 1])
+            landed(f.at[2:6, 34:36], recv_y.at[s, h, 1])
+
+    def sent_y(f, s, h):
+        @pl.when(g > 0)
+        def _():
+            landed(f.at[2:6, 2:4], send_y.at[s, h, 1])
+
+        @pl.when(g < G - 1)
+        def _():
+            landed(f.at[2:6, 32:34], send_y.at[s, h, 0])
 
     for h, quad in enumerate(QUADS):
         some = rb.at[h, :, 0:2 * (G - 1)]
@@ -312,14 +328,14 @@
                 fa2[pl.ds(((x + 2) * YE + 2) * 8 + zr, YB, stride=8), :] = turned[n * YB:(n + 1) * YB]
             return carry
 
-        lax.fori_loop(0, 8, turn, 0)
+        lax.fori_loop(0, 8, turn, 0, unroll=8)
         if h == 0:
             x_halo(fa, 0, begin)
-    y_halo(fa, 0, begin)
-
-    def z_edges(f):
+        y_halo(fa, 0, h)
+
+    def z_edges(f, x0, x1):
         def rows(ref, k):
-            return ref.reshape(ref.shape[0] * ref.shape[1] * 8, 128)[pl.ds(2 * YE * 8 + k, X * YE, stride=8), :]
+            return ref.reshape(ref.shape[0] * ref.shape[1] * 8, 128)[pl.ds((x0 + 2) * YE * 8 + k, (x1 - x0) * YE, stride=8), :]
 
         def static(k, n):
             return rows(coef.at[k], n)
@@ -332,21 +348,30 @@
         slope_next = minmod(jump, (next1 - next0) * pltpu.roll(static(OZ, 0), 96, 1))
         flux = face(last, next0, slope, slope_next, static(CZ, 7)) - mix[7:8, :] * jump
         for n, k, v in ((0, 7, next0), (0, 0, pltpu.roll(jump, 32, 1)), (1, 7, slope_next), (1, 0, pltpu.roll(flux, 32, 1))):
-            edge.at[n].reshape(X * YE * 8, 128)[pl.ds(k, X * YE, stride=8), :] = v
-
-    def advect(f):
-        z_edges(f)
+            edge.at[n].reshape(X * YE * 8, 128)[pl.ds(x0 * YE * 8 + k, (x1 - x0) * YE, stride=8), :] = v
+
+    def advect(f, h):
+        parts = [advect_part(f, x0, x1) for x0, x1 in RANGES[h]]
+
+        def column(y, carry):
+            return tuple(step(y, c) for (_, step), c in zip(parts, carry))
+
+        lax.fori_loop(0, YB, column, tuple(start for start, _ in parts), unroll=2)
+
+    def advect_part(f, x0, x1):
+        z_edges(f, x0, x1)
+        n = x1 - x0
 
         def cells(e):
-            return f[2:10, e]
+            return f[x0 + 2:x1 + 2, e]
 
         def along(k, e):
-            return coef[k, 2:10, e]
-
-        f1, f2 = cells(1), cells(2)
+            return coef[k, x0 + 2:x1 + 2, e]
+
         def open_y(e):
             return along(SEA, e) * along(SEA, e + 1)
 
+        f1, f2 = cells(1), cells(2)
         j0 = (f1 - cells(0)) * open_y(0)
         j1 = (f2 - f1) * open_y(1)
         j2 = (cells(3) - f2) * open_y(2)
@@ -356,29 +381,29 @@
         def column(y, carry):
             jump, slope, before = carry
             e = y + 2
-            fx = f[:, e]
-            inner, following = fx[2:10], cells(e + 1)
+            fx = f[x0:x1 + 4, e]
+            inner, following = fx[2:n + 2], cells(e + 1)
             jump_next = (cells(e + 2) - following) * open_y(e + 1)
             slope_next = minmod(jump, jump_next)
             after = face(inner, following, slope, slope_next, along(CY, e))
             total = inner - (after - before)
-            sea_x = coef[SEA, :, e]
+            sea_x = coef[SEA, x0:x1 + 4, e]
             jx = (fx[1:] - fx[:-1]) * (sea_x[1:] * sea_x[:-1])
             sx = minmod(jx[:-1], jx[1:])
-            flux = face(fx[1:10], fx[2:11], sx[:-1], sx[1:], coef[CX, 1:10, e])
+            flux = face(fx[1:n + 2], fx[2:n + 3], sx[:-1], sx[1:], coef[CX, x0 + 1:x1 + 2, e])
             total = total - (flux[1:] - flux[:-1])
-            edge0, edge1 = edge[0, :, e], edge[1, :, e]
+            edge0, edge1 = edge[0, x0:x1, e], edge[1, x0:x1, e]
             below = jnp.where(row == 7, edge0, pltpu.roll(inner, 7, 1))
             jz = (below - inner) * along(OZ, e)
             sz = minmod(jnp.where(row == 0, edge0, pltpu.roll(jz, 1, 1)), jz)
             sz_next = jnp.where(row == 7, edge1, pltpu.roll(sz, 7, 1))
             down = face(inner, below, sz, sz_next, along(CZ, e)) - mix[...] * jz
-            adv[:, y] = total - (down - jnp.where(row == 0, edge1, pltpu.roll(down, 1, 1)))
+            adv[x0:x1, y] = total - (down - jnp.where(row == 0, edge1, pltpu.roll(down, 1, 1)))
             return jump_next, slope_next, after
 
-        lax.fori_loop(0, YB, column, start)
-
-    def react(x, f):
+        return start, column
+
+    def react(x, result):
         a = adv[x]
         att = 0.05 + 0.1 * a * a
         inc = att
@@ -392,35 +417,19 @@
         both = jnp.dot(jnp.concatenate(halves(jnp.tanh(a).reshape(256, 128)), axis=1), wmat[...],
                        preferred_element_type=jnp.float32)
         response = (both[:, :128] + both[:, 128:]).reshape(YB, 8, 128)
-        f[x + 2, 2:34] = a + coef[SEA, x + 2, 2:34] * ((0.5 + light) * response)
-
-    arrive(fa, 0)
-    advect(fa)
-    for h, quad in enumerate(QUADS):
-        for x in quad:
-            react(x, fb)
-        if h == 0:
-            x_halo(fb, 1, begin)
-    y_halo(fb, 1, begin)
-    arrive(fb, 1)
-    advect(fb)
-    static_halo(lambda copy: copy.wait_send())
-    for s, f in ((0, fa), (1, fb)):
-        x_halo(f, s, lambda copy: copy.wait_send())
-        y_halo(f, s, lambda copy: copy.wait_send())
-
-    for h, quad in enumerate(QUADS):
-        for x in quad:
-            react(x, fa)
-
-        def turn_back(zr, carry, h=h, quad=quad):
-            stack = [fa2[pl.ds(((x + 2) * YE + 2) * 8 + zr, YB, stride=8), :] for x in quad]
+        result[...] = a + coef[SEA, x + 2, 2:34] * ((0.5 + light) * response)
+
+    fc2 = fc.reshape(X * YB * 8, 128)
+
+    def give_back(h, quad):
+        def turn_back(zr, carry):
+            stack = [fc2[pl.ds(x * YB * 8 + zr, YB, stride=8), :] for x in quad]
             so2[pl.ds(h * 4 * NT * 8 + zr, 128, stride=8), :] = jnp.concatenate(stack, axis=0).T
             return carry
 
-        lax.fori_loop(0, 8, turn_back, 0)
-
-        def send_back(d, carry, h=h):
+        lax.fori_loop(0, 8, turn_back, 0, unroll=8)
+
+        def send_back(d, carry):
             to = lax.rem(g + d, G)
             pltpu.make_async_remote_copy(
                 src_ref=so.at[h, :, pl.ds(2 * to, 2)], dst_ref=ro.at[h, g],
@@ -431,12 +440,36 @@
         lax.fori_loop(1, G, send_back, 0)
         pltpu.make_async_copy(so.at[h, :, pl.ds(2 * g, 2)], ro.at[h, g], local_sem.at[2 + h]).start()
 
+    arrive_x(fa, 0)
     for h, quad in enumerate(QUADS):
+        arrive_y(fa, 0, h)
+        advect(fa, h)
+        for x in quad:
+            react(x, fb.at[x + 2, 2:34])
+        if h == 0:
+            x_halo(fb, 1, begin)
+        y_halo(fb, 1, h)
+    for h in (1, 0):
+        if h == 0:
+            arrive_x(fb, 1)
+        arrive_y(fb, 1, h)
+        advect(fb, h)
+        for x in QUADS[h]:
+            react(x, fc.at[x])
+        give_back(h, QUADS[h])
+
+    static_halo(lambda copy: copy.wait_send())
+    for s, f in ((0, fa), (1, fb)):
+        x_halo(f, s, lambda copy: copy.wait_send())
+        for h in range(2):
+            sent_y(f, s, h)
+
+    for h in (1, 0):
         some = ro.at[h, 0:G - 1]
         pltpu.make_async_copy(some, some, recv_out.at[h]).wait()
         pltpu.make_async_copy(so.at[h, :, pl.ds(2 * g, 2)], ro.at[h, g], local_sem.at[2 + h]).wait()
 
-        def restore(n, carry, h=h, quad=quad):
+        def restore(n, carry, h=h, quad=QUADS[h]):
             t, zq = n // 4, n % 4
             for j in range(4):
                 v = block_swap([ro[h, 4 * j + i, zq, t] for i in range(4)], lane)
@@ -444,7 +477,7 @@
                     tout[j, pl.ds((t * NZ + zq * 8) * X + x, 8, stride=8), :] = b
             return carry
 
-        lax.fori_loop(0, 8, restore, 0)
+        lax.fori_loop(0, 8, restore, 0, unroll=4)
 
     for j in range(4):
         put(j).start()
@@ -465,9 +498,11 @@
     out = pl.pallas_call(
         kernel,
         out_shape=jax.ShapeDtypeStruct((2 * NZ * X, G * YB), f32),
-        in_specs=[anywhere] * 3 + [vmem, pl.BlockSpec(memory_space=pltpu.SMEM)],
+        in_specs=[anywhere] * 3 + [anywhere, anywhere],
         out_specs=anywhere,
         scratch_shapes=[
+            pltpu.VMEM((NT, NT), f32),
+            pltpu.SMEM((NZ,), f32),
             pltpu.VMEM((4, NC, 128, 128), jnp.bfloat16),
             pltpu.VMEM((2, XE * 48, 128), jnp.bfloat16),
             pltpu.VMEM((256, 128), jnp.bfloat16),
@@ -491,15 +526,16 @@
             pltpu.VMEM((XE, YE, 8, 128), f32),
             pltpu.VMEM((XE, YE, 8, 128), f32),
             pltpu.VMEM((X, YB, 8, 128), f32),
+            pltpu.VMEM((X, YB, 8, 128), f32),
             pltpu.VMEM((2, X, YE, 8, 128), f32),
             pltpu.VMEM((NC, XE, YE, 8, 128), f32),
             pltpu.VMEM((2, 4, NT, 8, 128), f32),
             pltpu.VMEM((2, G, 4, 2, 8, 128), f32),
-            dma((4,)), dma((3,)), dma((3,)),
-            dma((4,)), dma((4,)), dma((2,)), dma((2,)), dma((2, 4)), dma((2, 2)), dma((2, 2)), dma((2,)), dma((2,)), dma((4,)),
+            dma((6,)), dma((3,)), dma((3,)),
+            dma((4,)), dma((4,)), dma((2,)), dma((2,)), dma((2, 2)), dma((2, 2)), dma((2, 2, 2)), dma((2, 2, 2)), dma((2,)), dma((2,)), dma((4,)),
         ],
         compiler_params=pltpu.CompilerParams(
-            collective_id=0, has_side_effects=True, vmem_limit_bytes=48 * 2**20),
+            collective_id=0, has_side_effects=True, vmem_limit_bytes=60 * 2**20),
     )(tracers.reshape(2 * NZ * X, G * YB), velocity, sea_mask, coupling, mixing)
     return out.reshape(tracers.shape)
 

time: 68.3 us -> 57.6 us (0.84)
  the two profiles are of different devices: /device:TPU:37 before, /device:TPU:57 now
where the time goes in v4:
time: 57.6 us; the launch traced here: 57.5 us
  Pallas kernels  55.2 us (96%)
  local copies, waits for them, and re-layouts  2.26 us (4%)
    pallas_call x1, Pallas kernels, shards(): pl.pallas_call(kernel, out_shape=jax.ShapeDtypeStruct((2 * NZ * X, G * YB...  55.2 us
    unnamed x1, local copies, waits for them, and re-layouts  2.26 us

profile of v4, /device:TPU:57, one launch (start us, length us, event | category | flops | bytes accessed | tf_op | source)
XLA Modules:
  0.0 57.5 jit_solution(12097462334522969140)
XLA Ops:
  0.0 55.2 %shard_map.55 = f32[512,512]{1,0:T(8,128)} custom-call(f32[512,512]{1,0:T(8,128)} %bitcast.3, f32[3,32,8,32]{3,2,1,0:T(8,128)} %velocity.1, s32[32,8,512]{2,1,0:T(8,128)} %mask.1, f32[32,32]{1,0:T(8,128)} %coupling_in.1, f32[32]{0:T(128)} %mixing_in.1), custom_call_target="tpu_custom_call" | custom-call | tf_op jit(solution)/shard_map/pallas_call | solution.py:498
  55.2 2.3 %copy.7 = f32[2,32,8,512]{3,2,1,0:T(8,128)} copy(f32[2,32,8,512]{3,2,1,0:T(8,128)} %bitcast.2) | data formatting | bytes 2097152

commit v5 on v4

--- a/solution.py
+++ b/solution.py
@@ -45,11 +45,20 @@
 
 
 def kernel(tr, velocity, mask, coupling_in, mixing_in, out,
-           coupling, mixing, spread, stacked, own_mat, past_mat, mix, wmat, vel, sea3, q, dc, pack_up, pack_down, pack_y, got_low, got_high, got_y,
+           coupling, mixing, spread, stacked, own_mat, past_mat, mix, wmat, vel, vel_pack, vel_got, sea3, q, dc, pack_up, pack_down, pack_x, pack_y, got_x, got_low, got_high, got_y,
            tin, tout, sb, rb, fa, fb, fc, adv, edge, coef, so, ro,
            statics_in, send_static, recv_static,
            tiles_in, tiles_out, send_in, recv_in, send_halo, recv_x, send_y, recv_y, send_out, recv_out, local_sem):
     r, g = lax.axis_index("region"), lax.axis_index("group")
+    upper = lax.div(r, R // 2)
+
+    def flip(n, upper=upper):
+        return n + upper * (2 - 4 * lax.rem(lax.div(n, 2), 2))
+
+    block = flip(g)
+    other = g + 2 - 4 * lax.rem(lax.div(g, 2), 2)
+    g_next = jnp.where(r == R // 2 - 1, other, g)
+    g_last = jnp.where(r == R // 2, other, g)
     lane = lax.broadcasted_iota(jnp.int32, (8, 128), 1)
     row = lax.broadcasted_iota(jnp.int32, (8, 128), 0)
     fa2, fb2 = fa.reshape(XE * YE * 8, 128), fb.reshape(XE * YE * 8, 128)
@@ -61,7 +70,7 @@
     def put(j):
         return pltpu.make_async_copy(tout.at[j], out.at[:, pl.ds(j * 128, 128)], tiles_out.at[j])
 
-    at = lax.div(g, 4)
+    at = lax.div(block, 4)
     spots = (at, jnp.maximum(at - 1, 0), jnp.minimum(at + 1, 3))
     fetches = [pltpu.make_async_copy(velocity, vel, statics_in.at[0]),
                pltpu.make_async_copy(coupling_in, coupling, statics_in.at[4]),
@@ -90,11 +99,17 @@
 
     @pl.when(r > 0)
     def _():
-        pl.semaphore_signal(barrier, inc=1, device_id=(r - 1, g), device_id_type=MESH)
+        pl.semaphore_signal(barrier, inc=1, device_id=(r - 1, g_last), device_id_type=MESH)
+
+    @pl.when(r > R // 2)
+    def _():
+        pl.semaphore_signal(barrier, inc=1, device_id=(r - 1, other), device_id_type=MESH)
+
+    extra = jnp.where(jnp.logical_and(r >= R // 2, r < R - 1), 1, 0)
 
     @pl.when(r < R - 1)
     def _():
-        pl.semaphore_signal(barrier, inc=1, device_id=(r + 1, g), device_id_type=MESH)
+        pl.semaphore_signal(barrier, inc=1, device_id=(r + 1, g_next), device_id_type=MESH)
 
     for j in range(4):
         fetch(j).wait()
@@ -107,19 +122,48 @@
         def _():
             do(pltpu.make_async_remote_copy(
                 src_ref=pack_up, dst_ref=got_low, send_sem=send_static.at[0], recv_sem=recv_static.at[0],
-                device_id=(r + 1, g), device_id_type=MESH))
+                device_id=(r + 1, g_next), device_id_type=MESH))
 
         @pl.when(r > 0)
         def _():
             do(pltpu.make_async_remote_copy(
                 src_ref=pack_down, dst_ref=got_high, send_sem=send_static.at[1], recv_sem=recv_static.at[1],
-                device_id=(r - 1, g), device_id_type=MESH))
+                device_id=(r - 1, g_last), device_id_type=MESH))
+
+    def edges_over(do):
+        @pl.when(r < R - 1)
+        def _():
+            to = flip(g, lax.div(r + 1, R // 2))
+            do(pltpu.make_async_remote_copy(
+                src_ref=pack_x, dst_ref=got_x, send_sem=send_static.at[4], recv_sem=recv_static.at[4],
+                device_id=(r + 1, to), device_id_type=MESH))
 
         @pl.when(g < G - 1)
         def _():
             do(pltpu.make_async_remote_copy(
                 src_ref=pack_y, dst_ref=got_y, send_sem=send_static.at[2], recv_sem=recv_static.at[2],
-                device_id=(r, g + 1), device_id_type=MESH))
+                device_id=(r, flip(g + 1)), device_id_type=MESH))
+
+    def velocity_over(do, do_here):
+        @pl.when(upper > 0)
+        def _():
+            do(pltpu.make_async_remote_copy(
+                src_ref=vel_pack, dst_ref=vel_got, send_sem=send_static.at[3], recv_sem=recv_static.at[3],
+                device_id=(r, block), device_id_type=MESH))
+
+        @pl.when(upper == 0)
+        def _():
+            do_here(pltpu.make_async_copy(vel_pack, vel_got, recv_static.at[3]))
+
+    fetches[0].wait()
+    for k in range(3):
+        for m in range(8):
+            vel_pack[8 * k + m] = jnp.concatenate([vel[k, 4 * m + n] for n in range(4)], axis=1)
+    pack_x[...] = vel_pack.reshape(24 * X, 128)[pl.ds(7, 8, stride=8), :]
+    column = jnp.zeros((8, 128), jnp.float32)
+    for m in range(8):
+        column = jnp.where(lane % 32 == m, pltpu.roll(vel_pack[8 + m], m + 97, 1), column)
+    pack_y[...] = column
 
     for h, quad in enumerate(QUADS):
         def regroup(n, carry, h=h, quad=quad):
@@ -132,25 +176,32 @@
 
         lax.fori_loop(0, 8, regroup, 0, unroll=4)
         if h == 0:
-            pl.semaphore_wait(barrier, G - 1 + jnp.minimum(r, 1) + jnp.minimum(R - 1 - r, 1))
+            pl.semaphore_wait(barrier, G - 1 + jnp.minimum(r, 1) + jnp.minimum(R - 1 - r, 1) + extra)
+            velocity_over(begin, begin)
+            edges_over(begin)
 
         def send(d, carry, h=h):
             to = lax.rem(g + d, G)
             pltpu.make_async_remote_copy(
-                src_ref=sb.at[to, h], dst_ref=rb.at[h, :, pl.ds(2 * g, 2)],
+                src_ref=sb.at[flip(to), h], dst_ref=rb.at[h, :, pl.ds(2 * g, 2)],
                 send_sem=send_in.at[h], recv_sem=recv_in.at[h],
                 device_id=(r, to), device_id_type=MESH).start()
             return carry
 
         lax.fori_loop(1, G, send, 0)
-        pltpu.make_async_copy(sb.at[g, h], rb.at[h, :, pl.ds(2 * g, 2)], local_sem.at[h]).start()
+        pltpu.make_async_copy(sb.at[block, h], rb.at[h, :, pl.ds(2 * g, 2)], local_sem.at[h]).start()
 
     q[...] = jnp.zeros(q.shape, jnp.float32)
-    for copy in fetches:
+    for copy in fetches[1:]:
         copy.wait()
-    for k in range(3):
-        q[k, :, 2:10, 2:34] = vel[k]
-    place = lax.rem(g, 4)
+    velocity_over(lambda copy: copy.wait_recv(), lambda copy: copy.wait())
+    for n in range(4):
+        shifted = pltpu.roll(vel_got[...], (130 - 32 * n) % 128, 2)
+        shifted = jnp.where(jnp.logical_and(lane >= 2, lane < 34), shifted, 0.0)
+        for k in range(3):
+            for m in range(8):
+                q[k, 4 * m + n, 2:10, :] = shifted[8 * k + m]
+    place = lax.rem(block, 4)
     has_left = jnp.minimum(at, 1).astype(jnp.float32)
     has_right = jnp.minimum(3 - at, 1).astype(jnp.float32)
     centre = sea3[0].astype(jnp.float32)
@@ -166,13 +217,8 @@
     def put_rows(k, e, value):
         q.at[k].reshape(NZ * 16, 128)[pl.ds(e, NZ, stride=16), :] = value
 
-    pack_up[0], pack_up[1], pack_up[2] = level_rows(3, 8), level_rows(3, 9), level_rows(0, 9)
+    pack_up[0], pack_up[1] = level_rows(3, 8), level_rows(3, 9)
     pack_down[0], pack_down[1] = level_rows(3, 2), level_rows(3, 3)
-
-    def pack_level(z, p):
-        return jnp.where(lane == z, pltpu.roll(q[1, z, 2:10, :], lax.rem(z + 95, 128), 1), p)
-
-    pack_y[...] = lax.fori_loop(0, NZ, pack_level, jnp.zeros((8, 128), jnp.float32), unroll=8)
 
     static_halo(begin)
 
@@ -206,7 +252,10 @@
         pltpu.make_async_copy(got_low, got_low, recv_static.at[0]).wait()
         put_rows(3, 0, got_low[0])
         put_rows(3, 1, got_low[1])
-        put_rows(0, 1, got_low[2])
+        pltpu.make_async_copy(got_x, got_x, recv_static.at[4]).wait()
+        for n in range(4):
+            q.at[0].reshape(NZ * 16, 128)[pl.ds(n * 16 + 1, 8, stride=64), :] = jnp.where(
+                jnp.logical_and(lane >= 2, lane < 34), pltpu.roll(got_x[...], (130 - 32 * n) % 128, 1), 0.0)
 
     @pl.when(r < R - 1)
     def _():
@@ -214,13 +263,13 @@
         put_rows(3, 10, got_high[0])
         put_rows(3, 11, got_high[1])
 
-    @pl.when(g > 0)
+    @pl.when(block > 0)
     def _():
         pltpu.make_async_copy(got_y, got_y, recv_static.at[2]).wait()
 
         def unpack_level(z, carry):
             q[1, z, 2:10, :] = jnp.where(
-                lane == 1, pltpu.roll(got_y[...], lax.rem(129 - z, 128), 1), q[1, z, 2:10, :])
+                lane == 1, pltpu.roll(got_y[...], lax.rem(129 - lax.div(z, 4) - 32 * lax.rem(z, 4) + 128, 128), 1), q[1, z, 2:10, :])
             return carry
 
         lax.fori_loop(0, NZ, unpack_level, 0, unroll=8)
@@ -244,8 +293,6 @@
                 jnp.concatenate(rows, axis=0).T[:48].astype(jnp.bfloat16))
         return carry
 
-    lax.fori_loop(0, XE, stack_one, 0)
-
     def spread_one(zr, carry):
         for k in range(NC):
             wide = jnp.dot(stacked[zr // 4], spread[zr % 4, k], preferred_element_type=jnp.float32)
@@ -253,39 +300,37 @@
                 coef.at[k].reshape(XE * YE * 8, 128)[pl.ds(e * YE * 8 + zr, YE, stride=8), :] = wide[e * 48:e * 48 + YE]
         return carry
 
-    lax.fori_loop(0, 8, spread_one, 0)
-
     def x_halo(f, s, do):
         @pl.when(r > 0)
         def _():
             do(pltpu.make_async_remote_copy(
                 src_ref=f.at[2:4, 2:34], dst_ref=f.at[10:12, 2:34],
                 send_sem=send_halo.at[s, 0], recv_sem=recv_x.at[s, 1],
-                device_id=(r - 1, g), device_id_type=MESH))
+                device_id=(r - 1, g_last), device_id_type=MESH))
 
         @pl.when(r < R - 1)
         def _():
             do(pltpu.make_async_remote_copy(
                 src_ref=f.at[8:10, 2:34], dst_ref=f.at[0:2, 2:34],
                 send_sem=send_halo.at[s, 1], recv_sem=recv_x.at[s, 0],
-                device_id=(r + 1, g), device_id_type=MESH))
+                device_id=(r + 1, g_next), device_id_type=MESH))
 
     def y_halo(f, s, h):
-        @pl.when(g > 0)
+        @pl.when(block > 0)
         def _():
             for x0, x1 in RANGES[h]:
                 pltpu.make_async_remote_copy(
                     src_ref=f.at[x0 + 2:x1 + 2, 2:4], dst_ref=f.at[x0 + 2:x1 + 2, 34:36],
                     send_sem=send_y.at[s, h, 1], recv_sem=recv_y.at[s, h, 1],
-                    device_id=(r, g - 1), device_id_type=MESH).start()
-
-        @pl.when(g < G - 1)
+                    device_id=(r, flip(block - 1)), device_id_type=MESH).start()
+
+        @pl.when(block < G - 1)
         def _():
             for x0, x1 in RANGES[h]:
                 pltpu.make_async_remote_copy(
                     src_ref=f.at[x0 + 2:x1 + 2, 32:34], dst_ref=f.at[x0 + 2:x1 + 2, 0:2],
                     send_sem=send_y.at[s, h, 0], recv_sem=recv_y.at[s, h, 0],
-                    device_id=(r, g + 1), device_id_type=MESH).start()
+                    device_id=(r, flip(block + 1)), device_id_type=MESH).start()
 
     def landed(ref, sem):
         pltpu.make_async_copy(ref, ref, sem).wait()
@@ -300,27 +345,27 @@
             landed(f.at[10:12, 2:34], recv_x.at[s, 1])
 
     def arrive_y(f, s, h):
-        @pl.when(g > 0)
+        @pl.when(block > 0)
         def _():
             landed(f.at[2:6, 0:2], recv_y.at[s, h, 0])
 
-        @pl.when(g < G - 1)
+        @pl.when(block < G - 1)
         def _():
             landed(f.at[2:6, 34:36], recv_y.at[s, h, 1])
 
     def sent_y(f, s, h):
-        @pl.when(g > 0)
+        @pl.when(block > 0)
         def _():
             landed(f.at[2:6, 2:4], send_y.at[s, h, 1])
 
-        @pl.when(g < G - 1)
+        @pl.when(block < G - 1)
         def _():
             landed(f.at[2:6, 32:34], send_y.at[s, h, 0])
 
     for h, quad in enumerate(QUADS):
         some = rb.at[h, :, 0:2 * (G - 1)]
         pltpu.make_async_copy(some, some, recv_in.at[h]).wait()
-        pltpu.make_async_copy(sb.at[g, h], rb.at[h, :, pl.ds(2 * g, 2)], local_sem.at[h]).wait()
+        pltpu.make_async_copy(sb.at[block, h], rb.at[h, :, pl.ds(2 * g, 2)], local_sem.at[h]).wait()
 
         def turn(zr, carry, h=h, quad=quad):
             turned = rb2[pl.ds(h * 4 * NT * 8 + zr, 128, stride=8), :].T
@@ -332,6 +377,9 @@
         if h == 0:
             x_halo(fa, 0, begin)
         y_halo(fa, 0, h)
+        if h == 0:
+            lax.fori_loop(0, XE, stack_one, 0)
+            lax.fori_loop(0, 8, spread_one, 0)
 
     def z_edges(f, x0, x1):
         def rows(ref, k):
@@ -432,13 +480,13 @@
         def send_back(d, carry):
             to = lax.rem(g + d, G)
             pltpu.make_async_remote_copy(
-                src_ref=so.at[h, :, pl.ds(2 * to, 2)], dst_ref=ro.at[h, g],
+                src_ref=so.at[h, :, pl.ds(2 * to, 2)], dst_ref=ro.at[h, block],
                 send_sem=send_out.at[h], recv_sem=recv_out.at[h],
                 device_id=(r, to), device_id_type=MESH).start()
             return carry
 
         lax.fori_loop(1, G, send_back, 0)
-        pltpu.make_async_copy(so.at[h, :, pl.ds(2 * g, 2)], ro.at[h, g], local_sem.at[2 + h]).start()
+        pltpu.make_async_copy(so.at[h, :, pl.ds(2 * g, 2)], ro.at[h, block], local_sem.at[2 + h]).start()
 
     arrive_x(fa, 0)
     for h, quad in enumerate(QUADS):
@@ -459,6 +507,12 @@
         give_back(h, QUADS[h])
 
     static_halo(lambda copy: copy.wait_send())
+    edges_over(lambda copy: copy.wait_send())
+
+    @pl.when(upper > 0)
+    def _():
+        landed(vel_pack, send_static.at[3])
+
     for s, f in ((0, fa), (1, fb)):
         x_halo(f, s, lambda copy: copy.wait_send())
         for h in range(2):
@@ -467,7 +521,7 @@
     for h in (1, 0):
         some = ro.at[h, 0:G - 1]
         pltpu.make_async_copy(some, some, recv_out.at[h]).wait()
-        pltpu.make_async_copy(so.at[h, :, pl.ds(2 * g, 2)], ro.at[h, g], local_sem.at[2 + h]).wait()
+        pltpu.make_async_copy(so.at[h, :, pl.ds(2 * g, 2)], ro.at[h, block], local_sem.at[2 + h]).wait()
 
         def restore(n, carry, h=h, quad=QUADS[h]):
             t, zq = n // 4, n % 4
@@ -510,13 +564,17 @@
             pltpu.VMEM((8, 128), f32),
             pltpu.VMEM((256, 256), jnp.bfloat16),
             pltpu.VMEM((3, NZ, X, YB), f32),
+            pltpu.VMEM((24, X, 128), f32),
+            pltpu.VMEM((24, X, 128), f32),
             pltpu.VMEM((3, NZ, X, 128), jnp.int32),
             pltpu.VMEM((4, NZ, 16, 128), f32),
             pltpu.VMEM((8, NZ, 16, 128), f32),
-            pltpu.VMEM((3, NZ, 128), f32),
+            pltpu.VMEM((2, NZ, 128), f32),
             pltpu.VMEM((2, NZ, 128), f32),
             pltpu.VMEM((8, 128), f32),
-            pltpu.VMEM((3, NZ, 128), f32),
+            pltpu.VMEM((8, 128), f32),
+            pltpu.VMEM((8, 128), f32),
+            pltpu.VMEM((2, NZ, 128), f32),
             pltpu.VMEM((2, NZ, 128), f32),
             pltpu.VMEM((8, 128), f32),
             pltpu.VMEM((4, 2 * NZ * X, 128), f32),
@@ -531,7 +589,7 @@
             pltpu.VMEM((NC, XE, YE, 8, 128), f32),
             pltpu.VMEM((2, 4, NT, 8, 128), f32),
             pltpu.VMEM((2, G, 4, 2, 8, 128), f32),
-            dma((6,)), dma((3,)), dma((3,)),
+            dma((6,)), dma((5,)), dma((5,)),
             dma((4,)), dma((4,)), dma((2,)), dma((2,)), dma((2, 2)), dma((2, 2)), dma((2, 2, 2)), dma((2, 2, 2)), dma((2,)), dma((2,)), dma((4,)),
         ],
         compiler_params=pltpu.CompilerParams(

time: 57.6 us -> 56.1 us (0.974)
  Pallas kernels: 55.2 us -> 53.6 us
    pallas_call x1, Pallas kernels: 55.2 us -> 53.6 us  [shards(): pl.pallas_call(kernel, out_shape=jax.ShapeDtypeStruct((2 * NZ * X, G * YB...]
where the time goes in v5:
time: 56.1 us; the launch traced here: 55.9 us
  Pallas kernels  53.6 us (96%)
  local copies, waits for them, and re-layouts  2.26 us (4%)
    pallas_call x1, Pallas kernels, shards(): pl.pallas_call(kernel, out_shape=jax.ShapeDtypeStruct((2 * NZ * X, G * YB...  53.6 us
    unnamed x1, local copies, waits for them, and re-layouts  2.26 us

profile of v5, /device:TPU:57, one launch (start us, length us, event | category | flops | bytes accessed | tf_op | source)
XLA Modules:
  0.0 55.9 jit_solution(17842110725084905314)
XLA Ops:
  0.0 53.6 %shard_map.55 = f32[512,512]{1,0:T(8,128)} custom-call(f32[512,512]{1,0:T(8,128)} %bitcast.3, f32[3,32,8,32]{3,2,1,0:T(8,128)} %velocity.1, s32[32,8,512]{2,1,0:T(8,128)} %mask.1, f32[32,32]{1,0:T(8,128)} %coupling_in.1, f32[32]{0:T(128)} %mixing_in.1), custom_call_target="tpu_custom_call" | custom-call | tf_op jit(solution)/shard_map/pallas_call | solution.py:552
  53.6 2.3 %copy.7 = f32[2,32,8,512]{3,2,1,0:T(8,128)} copy(f32[2,32,8,512]{3,2,1,0:T(8,128)} %bitcast.2) | data formatting | bytes 2097152

commit v6 on v5

--- a/solution.py
+++ b/solution.py
@@ -227,12 +227,12 @@
 
     square = (128, 128)
     block_in, block_out = iota(square, 0) // 32, iota(square, 1) // 32
-    for level in range(4):
-        for k in range(NC):
-            base = 32 * level + (24 + 4 * (k - 3) if k >= 3 else 4 * k)
-            place_k = iota(square, 0) - (base + block_out)
-            hit = place_k == 0 if k >= 3 else jnp.logical_or(place_k == 0, place_k == 12)
-            spread[level, k] = jnp.where(hit, 1.0, 0.0).astype(jnp.bfloat16)
+    tall = (256, 128)
+    part_at, block_at = iota(tall, 0) % 32, iota(tall, 1) // 32
+    for k in range(NC):
+        place_k = part_at - (block_at + (24 + 4 * (k - 3) if k >= 3 else 4 * k))
+        hit = place_k == 0 if k >= 3 else jnp.logical_or(place_k == 0, place_k == 12)
+        spread[:, k * 128:(k + 1) * 128] = jnp.where(hit, 1.0, 0.0).astype(jnp.bfloat16)
     first = iota(square, 0) % 32 == 0
     own = jnp.where(jnp.logical_and(first, block_in == block_out), 1.0, 0.0).astype(jnp.bfloat16)
     past = jnp.where(jnp.logical_and(first, block_in < block_out), 1.0, 0.0).astype(jnp.bfloat16)
@@ -289,15 +289,19 @@
     def stack_one(e, carry):
         for half in range(2):
             rows = [dc.reshape(8 * NZ * 16, 128)[pl.ds((half * 4 + n) * 16 + e, 32, stride=128), :] for n in range(4)]
-            stacked[half, pl.ds(pl.multiple_of(e * 48, 16), 48), :] = (
-                jnp.concatenate(rows, axis=0).T[:48].astype(jnp.bfloat16))
+            stacked[pl.ds(pl.multiple_of(e * 40, 8), 40), half * 128:(half + 1) * 128] = (
+                jnp.concatenate(rows, axis=0).T[:40])
         return carry
 
-    def spread_one(zr, carry):
-        for k in range(NC):
-            wide = jnp.dot(stacked[zr // 4], spread[zr % 4, k], preferred_element_type=jnp.float32)
-            for e in range(XE):
-                coef.at[k].reshape(XE * YE * 8, 128)[pl.ds(e * YE * 8 + zr, YE, stride=8), :] = wide[e * 48:e * 48 + YE]
+    own_lanes = iota((8, 256), 0) == iota((8, 256), 1) // 32
+
+    def spread_some(n, carry):
+        value = stacked[pl.ds(pl.multiple_of(n * 160, 8), 160), :]
+        value = jnp.where(own_lanes, jnp.broadcast_to(value[:, None, :], (160, 8, 256)), 0.0)
+        wide = jnp.dot(value.reshape(1280, 256).astype(jnp.bfloat16), spread[...], preferred_element_type=jnp.float32)
+        for m in range(4):
+            for k in range(NC):
+                coef[k, 4 * n + m] = wide[m * 320:m * 320 + YE * 8, k * 128:(k + 1) * 128].reshape(YE, 8, 128)
         return carry
 
     def x_halo(f, s, do):
@@ -378,8 +382,8 @@
             x_halo(fa, 0, begin)
         y_halo(fa, 0, h)
         if h == 0:
-            lax.fori_loop(0, XE, stack_one, 0)
-            lax.fori_loop(0, 8, spread_one, 0)
+            lax.fori_loop(0, XE, stack_one, 0, unroll=2)
+            lax.fori_loop(0, XE // 4, spread_some, 0)
 
     def z_edges(f, x0, x1):
         def rows(ref, k):
@@ -451,21 +455,27 @@
 
         return start, column
 
-    def react(x, result):
-        a = adv[x]
+    def react(h, results):
+        count = 4 * YB
+        a = jnp.concatenate([adv[x0:x1].reshape((x1 - x0) * YB, 8, 128) for x0, x1 in RANGES[h]], axis=0)
         att = 0.05 + 0.1 * a * a
         inc = att
         for step in (1, 2, 4):
             inc = inc + jnp.where(row >= step, pltpu.roll(inc, step, 1), 0.0)
-        exc = (inc - att).reshape(256, 128)
-        ahead = jnp.dot(jnp.concatenate(halves(exc), axis=1), own_mat[...], preferred_element_type=jnp.float32)
-        past = jnp.dot(jnp.concatenate(halves(inc.reshape(256, 128)), axis=1), past_mat[...],
-                       preferred_element_type=jnp.float32).reshape(YB, 8, 128)
-        light = jnp.exp(-(ahead.reshape(YB, 8, 128) + past[:, 7:8, :]))
-        both = jnp.dot(jnp.concatenate(halves(jnp.tanh(a).reshape(256, 128)), axis=1), wmat[...],
-                       preferred_element_type=jnp.float32)
-        response = (both[:, :128] + both[:, 128:]).reshape(YB, 8, 128)
-        result[...] = a + coef[SEA, x + 2, 2:34] * ((0.5 + light) * response)
+
+        def spread_over(value, matrix):
+            parts = jnp.concatenate(halves(value.reshape(count * 8, 128)), axis=1)
+            return jnp.dot(parts, matrix[...], preferred_element_type=jnp.float32)
+
+        both = spread_over(jnp.tanh(a), wmat)
+        ahead = spread_over(inc - att, own_mat).reshape(count, 8, 128)
+        past = spread_over(inc, past_mat).reshape(count, 8, 128)
+        light = jnp.exp(-(ahead + past[:, 7:8, :]))
+        response = (both[:, :128] + both[:, 128:]).reshape(count, 8, 128)
+        change = (0.5 + light) * response
+        for n, (x, result) in enumerate(zip(QUADS[h], results)):
+            part = slice(n * YB, (n + 1) * YB)
+            result[...] = a[part] + coef[SEA, x + 2, 2:34] * change[part]
 
     fc2 = fc.reshape(X * YB * 8, 128)
 
@@ -488,12 +498,12 @@
         lax.fori_loop(1, G, send_back, 0)
         pltpu.make_async_copy(so.at[h, :, pl.ds(2 * g, 2)], ro.at[h, block], local_sem.at[2 + h]).start()
 
-    arrive_x(fa, 0)
-    for h, quad in enumerate(QUADS):
+    for h in (1, 0):
+        if h == 0:
+            arrive_x(fa, 0)
         arrive_y(fa, 0, h)
         advect(fa, h)
-        for x in quad:
-            react(x, fb.at[x + 2, 2:34])
+        react(h, [fb.at[x + 2, 2:34] for x in QUADS[h]])
         if h == 0:
             x_halo(fb, 1, begin)
         y_halo(fb, 1, h)
@@ -502,8 +512,7 @@
             arrive_x(fb, 1)
         arrive_y(fb, 1, h)
         advect(fb, h)
-        for x in QUADS[h]:
-            react(x, fc.at[x])
+        react(h, [fc.at[x] for x in QUADS[h]])
         give_back(h, QUADS[h])
 
     static_halo(lambda copy: copy.wait_send())
@@ -557,8 +566,8 @@
         scratch_shapes=[
             pltpu.VMEM((NT, NT), f32),
             pltpu.SMEM((NZ,), f32),
-            pltpu.VMEM((4, NC, 128, 128), jnp.bfloat16),
-            pltpu.VMEM((2, XE * 48, 128), jnp.bfloat16),
+            pltpu.VMEM((256, NC * 128), jnp.bfloat16),
+            pltpu.VMEM((XE * 40, 256), f32),
             pltpu.VMEM((256, 128), jnp.bfloat16),
             pltpu.VMEM((256, 128), jnp.bfloat16),
             pltpu.VMEM((8, 128), f32),

time: 56.1 us -> 54.9 us (0.979)
  Pallas kernels: 53.6 us -> 52.1 us
    pallas_call x1, Pallas kernels: 53.6 us -> 52.1 us  [shards(): pl.pallas_call(kernel, out_shape=jax.ShapeDtypeStruct((2 * NZ * X, G * YB...]
where the time goes in v6:
time: 54.9 us; the launch traced here: 54.4 us
  Pallas kernels  52.1 us (95%)
  local copies, waits for them, and re-layouts  2.26 us (4%)
    pallas_call x1, Pallas kernels, shards(): pl.pallas_call(kernel, out_shape=jax.ShapeDtypeStruct((2 * NZ * X, G * YB...  52.1 us
    unnamed x1, local copies, waits for them, and re-layouts  2.26 us

profile of v6, /device:TPU:57, one launch (start us, length us, event | category | flops | bytes accessed | tf_op | source)
XLA Modules:
  0.0 54.4 jit_solution(4224137890944217754)
XLA Ops:
  0.0 52.1 %shard_map.55 = f32[512,512]{1,0:T(8,128)} custom-call(f32[512,512]{1,0:T(8,128)} %bitcast.3, f32[3,32,8,32]{3,2,1,0:T(8,128)} %velocity.1, s32[32,8,512]{2,1,0:T(8,128)} %mask.1, f32[32,32]{1,0:T(8,128)} %coupling_in.1, f32[32]{0:T(128)} %mixing_in.1), custom_call_target="tpu_custom_call" | custom-call | tf_op jit(solution)/shard_map/pallas_call | solution.py:561
  52.1 2.3 %copy.7 = f32[2,32,8,512]{3,2,1,0:T(8,128)} copy(f32[2,32,8,512]{3,2,1,0:T(8,128)} %bitcast.2) | data formatting | bytes 2097152

commit v7 on v6

--- a/solution.py
+++ b/solution.py
@@ -304,20 +304,20 @@
                 coef[k, 4 * n + m] = wide[m * 320:m * 320 + YE * 8, k * 128:(k + 1) * 128].reshape(YE, 8, 128)
         return carry
 
-    def x_halo(f, s, do):
+    def x_halo(f, s, y0, y1):
         @pl.when(r > 0)
         def _():
-            do(pltpu.make_async_remote_copy(
-                src_ref=f.at[2:4, 2:34], dst_ref=f.at[10:12, 2:34],
+            pltpu.make_async_remote_copy(
+                src_ref=f.at[2:4, y0 + 2:y1 + 2], dst_ref=f.at[10:12, y0 + 2:y1 + 2],
                 send_sem=send_halo.at[s, 0], recv_sem=recv_x.at[s, 1],
-                device_id=(r - 1, g_last), device_id_type=MESH))
+                device_id=(r - 1, g_last), device_id_type=MESH).start()
 
         @pl.when(r < R - 1)
         def _():
-            do(pltpu.make_async_remote_copy(
-                src_ref=f.at[8:10, 2:34], dst_ref=f.at[0:2, 2:34],
+            pltpu.make_async_remote_copy(
+                src_ref=f.at[8:10, y0 + 2:y1 + 2], dst_ref=f.at[0:2, y0 + 2:y1 + 2],
                 send_sem=send_halo.at[s, 1], recv_sem=recv_x.at[s, 0],
-                device_id=(r + 1, g_next), device_id_type=MESH))
+                device_id=(r + 1, g_next), device_id_type=MESH).start()
 
     def y_halo(f, s, h):
         @pl.when(block > 0)
@@ -339,6 +339,15 @@
     def landed(ref, sem):
         pltpu.make_async_copy(ref, ref, sem).wait()
 
+    def sent_x(f, s):
+        @pl.when(r > 0)
+        def _():
+            landed(f.at[2:4, 2:34], send_halo.at[s, 0])
+
+        @pl.when(r < R - 1)
+        def _():
+            landed(f.at[8:10, 2:34], send_halo.at[s, 1])
+
     def arrive_x(f, s):
         @pl.when(r > 0)
         def _():
@@ -379,11 +388,10 @@
 
         lax.fori_loop(0, 8, turn, 0, unroll=8)
         if h == 0:
-            x_halo(fa, 0, begin)
+            x_halo(fa, 0, 0, YB)
         y_halo(fa, 0, h)
         if h == 0:
             lax.fori_loop(0, XE, stack_one, 0, unroll=2)
-            lax.fori_loop(0, XE // 4, spread_some, 0)
 
     def z_edges(f, x0, x1):
         def rows(ref, k):
@@ -402,13 +410,16 @@
         for n, k, v in ((0, 7, next0), (0, 0, pltpu.roll(jump, 32, 1)), (1, 7, slope_next), (1, 0, pltpu.roll(flux, 32, 1))):
             edge.at[n].reshape(X * YE * 8, 128)[pl.ds(x0 * YE * 8 + k, (x1 - x0) * YE, stride=8), :] = v
 
-    def advect(f, h):
+    def advect(f, h, then):
         parts = [advect_part(f, x0, x1) for x0, x1 in RANGES[h]]
 
         def column(y, carry):
             return tuple(step(y, c) for (_, step), c in zip(parts, carry))
 
-        lax.fori_loop(0, YB, column, tuple(start for start, _ in parts), unroll=2)
+        carry = tuple(start for start, _ in parts)
+        for y0, y1 in ((0, YB // 2), (YB // 2, YB)):
+            carry = lax.fori_loop(y0, y1, column, carry, unroll=4)
+            then(y0, y1)
 
     def advect_part(f, x0, x1):
         z_edges(f, x0, x1)
@@ -455,9 +466,10 @@
 
         return start, column
 
-    def react(h, results):
-        count = 4 * YB
-        a = jnp.concatenate([adv[x0:x1].reshape((x1 - x0) * YB, 8, 128) for x0, x1 in RANGES[h]], axis=0)
+    def react(h, results, y0, y1):
+        length = y1 - y0
+        count = 4 * length
+        a = jnp.concatenate([adv[x0:x1, y0:y1].reshape((x1 - x0) * length, 8, 128) for x0, x1 in RANGES[h]], axis=0)
         att = 0.05 + 0.1 * a * a
         inc = att
         for step in (1, 2, 4):
@@ -474,8 +486,8 @@
         response = (both[:, :128] + both[:, 128:]).reshape(count, 8, 128)
         change = (0.5 + light) * response
         for n, (x, result) in enumerate(zip(QUADS[h], results)):
-            part = slice(n * YB, (n + 1) * YB)
-            result[...] = a[part] + coef[SEA, x + 2, 2:34] * change[part]
+            part = slice(n * length, (n + 1) * length)
+            result[...] = a[part] + coef[SEA, x + 2, y0 + 2:y1 + 2] * change[part]
 
     fc2 = fc.reshape(X * YB * 8, 128)
 
@@ -498,21 +510,29 @@
         lax.fori_loop(1, G, send_back, 0)
         pltpu.make_async_copy(so.at[h, :, pl.ds(2 * g, 2)], ro.at[h, block], local_sem.at[2 + h]).start()
 
+    lax.fori_loop(0, XE // 4, spread_some, 0)
+
     for h in (1, 0):
         if h == 0:
             arrive_x(fa, 0)
         arrive_y(fa, 0, h)
-        advect(fa, h)
-        react(h, [fb.at[x + 2, 2:34] for x in QUADS[h]])
-        if h == 0:
-            x_halo(fb, 1, begin)
+
+        def step_1(y0, y1, h=h):
+            if h == 1:
+                if y1 == YB:
+                    react(h, [fb.at[x + 2, 2:34] for x in QUADS[h]], 0, YB)
+            else:
+                react(h, [fb.at[x + 2, y0 + 2:y1 + 2] for x in QUADS[h]], y0, y1)
+                x_halo(fb, 1, y0, y1)
+
+        advect(fa, h, step_1)
         y_halo(fb, 1, h)
     for h in (1, 0):
         if h == 0:
             arrive_x(fb, 1)
         arrive_y(fb, 1, h)
-        advect(fb, h)
-        react(h, [fc.at[x] for x in QUADS[h]])
+        advect(fb, h, lambda y0, y1: None)
+        react(h, [fc.at[x] for x in QUADS[h]], 0, YB)
         give_back(h, QUADS[h])
 
     static_halo(lambda copy: copy.wait_send())
@@ -523,7 +543,7 @@
         landed(vel_pack, send_static.at[3])
 
     for s, f in ((0, fa), (1, fb)):
-        x_halo(f, s, lambda copy: copy.wait_send())
+        sent_x(f, s)
         for h in range(2):
             sent_y(f, s, h)
 

time: 54.9 us -> 53.1 us (0.967)
  Pallas kernels: 52.1 us -> 50.6 us
    pallas_call x1, Pallas kernels: 52.1 us -> 50.6 us  [shards(): pl.pallas_call(kernel, out_shape=jax.ShapeDtypeStruct((2 * NZ * X, G * YB...]
where the time goes in v7:
time: 53.1 us; the launch traced here: 52.9 us
  Pallas kernels  50.6 us (95%)
  local copies, waits for them, and re-layouts  2.26 us (4%)
    pallas_call x1, Pallas kernels, shards(): pl.pallas_call(kernel, out_shape=jax.ShapeDtypeStruct((2 * NZ * X, G * YB...  50.6 us
    unnamed x1, local copies, waits for them, and re-layouts  2.26 us

profile of v7, /device:TPU:57, one launch (start us, length us, event | category | flops | bytes accessed | tf_op | source)
XLA Modules:
  0.0 52.9 jit_solution(18108219581703068099)
XLA Ops:
  0.0 50.6 %shard_map.55 = f32[512,512]{1,0:T(8,128)} custom-call(f32[512,512]{1,0:T(8,128)} %bitcast.3, f32[3,32,8,32]{3,2,1,0:T(8,128)} %velocity.1, s32[32,8,512]{2,1,0:T(8,128)} %mask.1, f32[32,32]{1,0:T(8,128)} %coupling_in.1, f32[32]{0:T(128)} %mixing_in.1), custom_call_target="tpu_custom_call" | custom-call | tf_op jit(solution)/shard_map/pallas_call | solution.py:581
  50.6 2.3 %copy.7 = f32[2,32,8,512]{3,2,1,0:T(8,128)} copy(f32[2,32,8,512]{3,2,1,0:T(8,128)} %bitcast.2) | data formatting | bytes 2097152

commit v8 on v7

--- a/solution.py
+++ b/solution.py
@@ -305,18 +305,20 @@
         return carry
 
     def x_halo(f, s, y0, y1):
+        slot = s + y0 // (YB // 2)
+
         @pl.when(r > 0)
         def _():
             pltpu.make_async_remote_copy(
                 src_ref=f.at[2:4, y0 + 2:y1 + 2], dst_ref=f.at[10:12, y0 + 2:y1 + 2],
-                send_sem=send_halo.at[s, 0], recv_sem=recv_x.at[s, 1],
+                send_sem=send_halo.at[s, 0], recv_sem=recv_x.at[slot, 1],
                 device_id=(r - 1, g_last), device_id_type=MESH).start()
 
         @pl.when(r < R - 1)
         def _():
             pltpu.make_async_remote_copy(
                 src_ref=f.at[8:10, y0 + 2:y1 + 2], dst_ref=f.at[0:2, y0 + 2:y1 + 2],
-                send_sem=send_halo.at[s, 1], recv_sem=recv_x.at[s, 0],
+                send_sem=send_halo.at[s, 1], recv_sem=recv_x.at[slot, 0],
                 device_id=(r + 1, g_next), device_id_type=MESH).start()
 
     def y_halo(f, s, h):
@@ -348,14 +350,16 @@
         def _():
             landed(f.at[8:10, 2:34], send_halo.at[s, 1])
 
-    def arrive_x(f, s):
+    def arrive_x(f, s, y0, y1):
+        slot = s + y0 // (YB // 2)
+
         @pl.when(r > 0)
         def _():
-            landed(f.at[0:2, 2:34], recv_x.at[s, 0])
+            landed(f.at[0:2, y0 + 2:y1 + 2], recv_x.at[slot, 0])
 
         @pl.when(r < R - 1)
         def _():
-            landed(f.at[10:12, 2:34], recv_x.at[s, 1])
+            landed(f.at[10:12, y0 + 2:y1 + 2], recv_x.at[slot, 1])
 
     def arrive_y(f, s, h):
         @pl.when(block > 0)
@@ -410,7 +414,7 @@
         for n, k, v in ((0, 7, next0), (0, 0, pltpu.roll(jump, 32, 1)), (1, 7, slope_next), (1, 0, pltpu.roll(flux, 32, 1))):
             edge.at[n].reshape(X * YE * 8, 128)[pl.ds(x0 * YE * 8 + k, (x1 - x0) * YE, stride=8), :] = v
 
-    def advect(f, h, then):
+    def advect(f, h, then, ready):
         parts = [advect_part(f, x0, x1) for x0, x1 in RANGES[h]]
 
         def column(y, carry):
@@ -418,6 +422,7 @@
 
         carry = tuple(start for start, _ in parts)
         for y0, y1 in ((0, YB // 2), (YB // 2, YB)):
+            ready(y0, y1)
             carry = lax.fori_loop(y0, y1, column, carry, unroll=4)
             then(y0, y1)
 
@@ -514,7 +519,7 @@
 
     for h in (1, 0):
         if h == 0:
-            arrive_x(fa, 0)
+            arrive_x(fa, 0, 0, YB)
         arrive_y(fa, 0, h)
 
         def step_1(y0, y1, h=h):
@@ -525,13 +530,11 @@
                 react(h, [fb.at[x + 2, y0 + 2:y1 + 2] for x in QUADS[h]], y0, y1)
                 x_halo(fb, 1, y0, y1)
 
-        advect(fa, h, step_1)
+        advect(fa, h, step_1, lambda y0, y1: None)
         y_halo(fb, 1, h)
     for h in (1, 0):
-        if h == 0:
-            arrive_x(fb, 1)
         arrive_y(fb, 1, h)
-        advect(fb, h, lambda y0, y1: None)
+        advect(fb, h, lambda y0, y1: None, lambda y0, y1, h=h: arrive_x(fb, 1, y0, y1) if h == 0 else None)
         react(h, [fc.at[x] for x in QUADS[h]], 0, YB)
         give_back(h, QUADS[h])
 
@@ -619,7 +622,7 @@
             pltpu.VMEM((2, 4, NT, 8, 128), f32),
             pltpu.VMEM((2, G, 4, 2, 8, 128), f32),
             dma((6,)), dma((5,)), dma((5,)),
-            dma((4,)), dma((4,)), dma((2,)), dma((2,)), dma((2, 2)), dma((2, 2)), dma((2, 2, 2)), dma((2, 2, 2)), dma((2,)), dma((2,)), dma((4,)),
+            dma((4,)), dma((4,)), dma((2,)), dma((2,)), dma((2, 2)), dma((3, 2)), dma((2, 2, 2)), dma((2, 2, 2)), dma((2,)), dma((2,)), dma((4,)),
         ],
         compiler_params=pltpu.CompilerParams(
             collective_id=0, has_side_effects=True, vmem_limit_bytes=60 * 2**20),

time: 53.1 us -> 52.2 us (0.983)
  Pallas kernels: 50.6 us -> 49.7 us
    pallas_call x1, Pallas kernels: 50.6 us -> 49.7 us  [shards(): pl.pallas_call(kernel, out_shape=jax.ShapeDtypeStruct((2 * NZ * X, G * YB...]
where the time goes in v8:
time: 52.2 us; the launch traced here: 52 us
  Pallas kernels  49.7 us (95%)
  local copies, waits for them, and re-layouts  2.26 us (4%)
    pallas_call x1, Pallas kernels, shards(): pl.pallas_call(kernel, out_shape=jax.ShapeDtypeStruct((2 * NZ * X, G * YB...  49.7 us
    unnamed x1, local copies, waits for them, and re-layouts  2.26 us

profile of v8, /device:TPU:57, one launch (start us, length us, event | category | flops | bytes accessed | tf_op | source)
XLA Modules:
  0.0 52.0 jit_solution(5160955993674692292)
XLA Ops:
  0.0 49.7 %shard_map.55 = f32[512,512]{1,0:T(8,128)} custom-call(f32[512,512]{1,0:T(8,128)} %bitcast.3, f32[3,32,8,32]{3,2,1,0:T(8,128)} %velocity.1, s32[32,8,512]{2,1,0:T(8,128)} %mask.1, f32[32,32]{1,0:T(8,128)} %coupling_in.1, f32[32]{0:T(128)} %mixing_in.1), custom_call_target="tpu_custom_call" | custom-call | tf_op jit(solution)/shard_map/pallas_call | solution.py:584
  49.7 2.3 %copy.7 = f32[2,32,8,512]{3,2,1,0:T(8,128)} copy(f32[2,32,8,512]{3,2,1,0:T(8,128)} %bitcast.2) | data formatting | bytes 2097152

commit v9 on v8

--- a/solution.py
+++ b/solution.py
@@ -518,8 +518,6 @@
     lax.fori_loop(0, XE // 4, spread_some, 0)
 
     for h in (1, 0):
-        if h == 0:
-            arrive_x(fa, 0, 0, YB)
         arrive_y(fa, 0, h)
 
         def step_1(y0, y1, h=h):
@@ -530,7 +528,7 @@
                 react(h, [fb.at[x + 2, y0 + 2:y1 + 2] for x in QUADS[h]], y0, y1)
                 x_halo(fb, 1, y0, y1)
 
-        advect(fa, h, step_1, lambda y0, y1: None)
+        advect(fa, h, step_1, lambda y0, y1, h=h: arrive_x(fa, 0, 0, YB) if h == 0 and y0 == 0 else None)
         y_halo(fb, 1, h)
     for h in (1, 0):
         arrive_y(fb, 1, h)

time: 52.2 us -> 51.9 us (level)
  no operation moved by 1% of the time
where the time goes in v9:
time: 51.9 us; the launch traced here: 51.6 us
  Pallas kernels  49.3 us (95%)
  local copies, waits for them, and re-layouts  2.26 us (4%)
    pallas_call x1, Pallas kernels, shards(): pl.pallas_call(kernel, out_shape=jax.ShapeDtypeStruct((2 * NZ * X, G * YB...  49.3 us
    unnamed x1, local copies, waits for them, and re-layouts  2.26 us

profile of v9, /device:TPU:57, one launch (start us, length us, event | category | flops | bytes accessed | tf_op | source)
XLA Modules:
  0.0 51.6 jit_solution(4616746261869262911)
XLA Ops:
  0.0 49.3 %shard_map.55 = f32[512,512]{1,0:T(8,128)} custom-call(f32[512,512]{1,0:T(8,128)} %bitcast.3, f32[3,32,8,32]{3,2,1,0:T(8,128)} %velocity.1, s32[32,8,512]{2,1,0:T(8,128)} %mask.1, f32[32,32]{1,0:T(8,128)} %coupling_in.1, f32[32]{0:T(128)} %mixing_in.1), custom_call_target="tpu_custom_call" | custom-call | tf_op jit(solution)/shard_map/pallas_call | solution.py:582
  49.3 2.3 %copy.7 = f32[2,32,8,512]{3,2,1,0:T(8,128)} copy(f32[2,32,8,512]{3,2,1,0:T(8,128)} %bitcast.2) | data formatting | bytes 2097152

commit v10 on v9

--- a/solution.py
+++ b/solution.py
@@ -174,7 +174,7 @@
                     sb[4 * j + i, h, zq, t] = b
             return carry
 
-        lax.fori_loop(0, 8, regroup, 0, unroll=4)
+        lax.fori_loop(0, 8, regroup, 0, unroll=8)
         if h == 0:
             pl.semaphore_wait(barrier, G - 1 + jnp.minimum(r, 1) + jnp.minimum(R - 1 - r, 1) + extra)
             velocity_over(begin, begin)

time: 51.9 us -> 52.7 us (1.015)
  Pallas kernels: 49.3 us -> 49.9 us
    pallas_call x1, Pallas kernels: 49.3 us -> 49.9 us  [shards(): pl.pallas_call(kernel, out_shape=jax.ShapeDtypeStruct((2 * NZ * X, G * YB...]
where the time goes in v10:
time: 52.7 us; the launch traced here: 52.1 us
  Pallas kernels  49.9 us (95%)
  local copies, waits for them, and re-layouts  2.26 us (4%)
    pallas_call x1, Pallas kernels, shards(): pl.pallas_call(kernel, out_shape=jax.ShapeDtypeStruct((2 * NZ * X, G * YB...  49.9 us
    unnamed x1, local copies, waits for them, and re-layouts  2.26 us

profile of v10, /device:TPU:57, one launch (start us, length us, event | category | flops | bytes accessed | tf_op | source)
XLA Modules:
  0.0 52.1 jit_solution(17222025204790916346)
XLA Ops:
  0.0 49.9 %shard_map.55 = f32[512,512]{1,0:T(8,128)} custom-call(f32[512,512]{1,0:T(8,128)} %bitcast.3, f32[3,32,8,32]{3,2,1,0:T(8,128)} %velocity.1, s32[32,8,512]{2,1,0:T(8,128)} %mask.1, f32[32,32]{1,0:T(8,128)} %coupling_in.1, f32[32]{0:T(128)} %mixing_in.1), custom_call_target="tpu_custom_call" | custom-call | tf_op jit(solution)/shard_map/pallas_call | solution.py:582
  49.9 2.3 %copy.7 = f32[2,32,8,512]{3,2,1,0:T(8,128)} copy(f32[2,32,8,512]{3,2,1,0:T(8,128)} %bitcast.2) | data formatting | bytes 2097152
